TPU v7x, 256 devices: a whole 4x4x8 slice. The times are simulated.
256 devices in a mesh: phase: 4 (over y), rep: 8 (over z), tp: 8 (over x, core).
Axes of the slice: x: 4, y: 4, z: 8, core: 2. Of those that a mesh axis runs over, the one named last changes fastest.
Arguments:
- patches: bfloat16 [32768, 1280], P(('phase', 'rep')), may hold values from -160 to 160
- window_order: int32 [32, 1024], P(('phase', 'rep')), may hold values from 0 to 1023, each once within a row
- vis_gain: float32 [1280], replicated, may hold values from 0.5 to 1.5
- vis_qkv: bfloat16 [1280, 3840], P(None, 'tp'), may hold values from -0.15625 to 0.15625
- vis_qkv_bias: float32 [3840], P('tp'), may hold values from -6 to 6
- vis_proj: bfloat16 [1280, 1280], P('tp'), may hold values from -0.625 to 0.625
- vis_proj_bias: float32 [1280], replicated, may hold values from -3 to 3
- merge_gain: float32 [1280], replicated, may hold values from 0.5 to 1.5
- img_owner: int32 [32, 16], P(('phase', 'rep')), may hold values from 0 to 31, as said below
- img_slot: int32 [32, 16], P(('phase', 'rep')), may hold values from 0 to 31, as said below
- prompt_rows: bfloat16 [16384, 8192], P(('phase', 'rep'), 'tp'), may hold values from -160 to 160
- lang_gain: float32 [8192], replicated, may hold values from 0.5 to 1.5
- w_query: bfloat16 [8192, 4096], P(('phase', 'rep'), 'tp'), may hold values from -0.0625 to 0.0625
- b_query: float32 [4096], P('tp'), may hold values from -6 to 6
- w_key: bfloat16 [8192, 1024], P(('phase', 'rep'), 'tp'), may hold values from -0.0625 to 0.0625
- b_key: float32 [1024], P('tp'), may hold values from -6 to 6
- w_value: bfloat16 [8192, 1024], P(('phase', 'rep'), 'tp'), may hold values from -0.0625 to 0.0625
- b_value: float32 [1024], P('tp'), may hold values from -2.5 to 2.5
- page_owner: int32 [32, 16], P(('phase', 'rep')), may hold values from 0 to 7, as said below
- page_slot: int32 [32, 16], P(('phase', 'rep')), may hold values from 0 to 15, as said below
Outputs:
- image_buffer: bfloat16 [16384, 5120], P(('phase', 'rep'), 'tp')
- attn_out: bfloat16 [16384, 4096], P(('phase', 'rep'), 'tp')
- kv_pool: bfloat16 [512, 32, 2048], P(('phase', 'rep'), None, 'tp')
Inputs may be any that keep to these rules, and one draw needn't show every extreme that they name: `window_order`: each row lists every index of its block once. `img_owner`: the 16 requests of one block go to distinct owners; an owner receives at most 32 requests in all, and some owner exactly 32. `img_slot`: requests sent to one owner take distinct slots. `page_owner`: each block holds 4 prompts of whole pages, each prompt's pages going to one owner and the prompts of a block to distinct owners; within one phase every block has the same prompt lengths in the same order, 5, 5, 3 and 3 pages in an order drawn for the phase, so at most 5 pages go from one block to one owner, and every owner receives exactly 16 pages. `page_slot`: the pages that reach one owner take distinct slots.
All inputs are finite; a program needn't handle non-finite values.
Results may differ from a plain program's by a relative error of at most 0.013.
Values may be sent and summed in bfloat16 or wider, within the bound.
No kernel may reach another device: no remote copies, remote signals or barrier semaphores. Data moves between devices by JAX's collectives and lax.ppermute only.
A program may use at most 128 MiB of HBM per device.

v0:
```python
import jax
import jax.numpy as jnp
from jax import lax
from jax.experimental import pallas as pl
from jax.experimental.pallas import tpu as pltpu
from jax.sharding import PartitionSpec as P

VD = 1280
VHD = 80
LANE = 128
HD = 128
EPS = 1e-06
CAP = 5
UNIT = 256
LABEL_ROWS = 16
WINDOW = 384
VMEM_LIMIT = 56 * 1024 * 1024


def whole(shape):
    return pl.BlockSpec(shape, lambda *_: (0,) * len(shape))


def params(limit=VMEM_LIMIT):
    return pltpu.CompilerParams(vmem_limit_bytes=limit)


def shift(axis, by):
    n = lax.axis_size(axis)
    return lambda a: lax.ppermute(a, axis, [(i, (i + by) % n) for i in range(n)])


def spread_columns(count):
    shape = (count * VHD, count * LANE)
    source = lax.broadcasted_iota(jnp.int32, shape, 0)
    target = lax.broadcasted_iota(jnp.int32, shape, 1)
    inside = target & (LANE - 1)
    hit = (inside < VHD) & (source == (target >> 7) * VHD + inside)
    return jnp.where(hit, 1.0, 0.0).astype(jnp.bfloat16)


def spread_rows(count):
    shape = (count * LANE, count * VHD)
    target = lax.broadcasted_iota(jnp.int32, shape, 0)
    source = lax.broadcasted_iota(jnp.int32, shape, 1)
    inside = target & (LANE - 1)
    hit = (inside < VHD) & (source == (target >> 7) * VHD + inside)
    return jnp.where(hit, 1.0, 0.0).astype(jnp.bfloat16)


def vision_kernel(
    own_ref, order_ref, patches_ref, gain_ref, w_ref, bias_ref, proj_ref, keep_ref, send_ref,
    resid_ref, w_pad, proj_pad, held,
):
    parts, span, width = held.shape
    total = parts * span
    chunks = w_ref.shape[1] // VHD
    core, chip = own_ref[0], own_ref[1]

    @pl.when(pl.program_id(0) == 0)
    def _():
        w_pad[...] = jnp.dot(
            w_ref[...], spread_columns(chunks), preferred_element_type=jnp.float32
        ).astype(jnp.bfloat16)
        proj_pad[...] = jnp.dot(
            spread_rows(chunks // 3), proj_ref[...], preferred_element_type=jnp.float32
        ).astype(jnp.bfloat16)

    places = patches_ref.shape[0]
    wanted = order_ref[...].reshape(total, 1)
    onehot = jnp.where(
        wanted == lax.broadcasted_iota(jnp.int32, (total, places), 1), 1.0, 0.0
    ).astype(jnp.bfloat16)
    rows = jnp.dot(onehot, patches_ref[...], preferred_element_type=jnp.float32)
    held[...] = rows.astype(jnp.bfloat16).reshape(parts, span, width)
    half = width // 2
    mine = pl.multiple_of(core * half, LANE)
    other = pl.multiple_of((1 - core) * half, LANE)
    resid_ref[...] = held[chip, :, pl.ds(mine, half)]
    factor = lax.rsqrt(jnp.mean(rows * rows, axis=-1, keepdims=True) + EPS)
    normed = (rows * factor * gain_ref[...]).astype(jnp.bfloat16)
    projected = jnp.dot(normed, w_pad[...], preferred_element_type=jnp.float32) + bias_ref[...]
    projected = projected.astype(jnp.bfloat16)
    window_q = lax.broadcasted_iota(jnp.int32, (total, total), 0) % span // 16
    window_k = lax.broadcasted_iota(jnp.int32, (total, total), 1) % span // 16
    same = window_q == window_k
    heads = []
    for head in range(chunks // 3):
        at = head * 3 * LANE
        query = projected[:, at : at + LANE]
        keyed = projected[:, at + LANE : at + 2 * LANE]
        valued = projected[:, at + 2 * LANE : at + 3 * LANE]
        scores = lax.dot_general(
            query, keyed, (((1,), (1,)), ((), ())), preferred_element_type=jnp.float32
        ) * (VHD ** (-0.5))
        scores = jnp.where(same, scores, -1e30)
        raised = jnp.exp(scores - jnp.max(scores, axis=-1, keepdims=True))
        weights = (raised / jnp.sum(raised, axis=-1, keepdims=True)).astype(jnp.bfloat16)
        heads.append(
            jnp.dot(weights, valued, preferred_element_type=jnp.float32).astype(jnp.bfloat16)
        )
    mixed = jnp.concatenate(heads, axis=1)
    for out_ref, at in ((keep_ref, mine), (send_ref, other)):
        part = jnp.dot(mixed, proj_pad[:, pl.ds(at, half)], preferred_element_type=jnp.float32)
        out_ref[...] = part.astype(jnp.bfloat16).reshape(parts, span, half)


def vision_partial(order, patches, gain, w, bias_pad, proj, own):
    parts, span, _ = order.shape
    width = patches.shape[1]
    step = 64
    half = width // 2
    chunks = w.shape[1] // VHD
    spec = pl.BlockSpec((parts, step, half), lambda i, _: (0, i, 0))
    out = jax.ShapeDtypeStruct((parts, span, half), jnp.bfloat16)
    return pl.pallas_call(
        vision_kernel,
        grid_spec=pltpu.PrefetchScalarGridSpec(
            num_scalar_prefetch=1,
            grid=(span // step,),
            in_specs=[
                pl.BlockSpec((parts, step, 1), lambda i, _: (0, i, 0)),
                whole(patches.shape),
                whole(gain.shape),
                whole(w.shape),
                whole(bias_pad.shape),
                whole(proj.shape),
            ],
            out_specs=[spec, spec, pl.BlockSpec((step, half), lambda i, _: (i, 0))],
            scratch_shapes=[
                pltpu.VMEM((width, chunks * LANE), jnp.bfloat16),
                pltpu.VMEM((chunks // 3 * LANE, width), jnp.bfloat16),
                pltpu.VMEM((parts, step, width), jnp.bfloat16),
            ],
        ),
        out_shape=[out, out, jax.ShapeDtypeStruct((span, half), jnp.bfloat16)],
        compiler_params=params(),
        cost_estimate=pl.CostEstimate(
            flops=10_000_000_000, bytes_accessed=8_000_000, transcendentals=0
        ),
    )(own, order, patches, gain, w, bias_pad, proj)


def join_kernel(*refs):
    out_ref = refs[-1]
    at = 0
    for ref in refs[:-1]:
        out_ref[at : at + ref.shape[0]] = ref[...]
        at += ref.shape[0]


def join(*parts):
    shape = (sum(part.shape[0] for part in parts),) + parts[0].shape[1:]
    return pl.pallas_call(
        join_kernel,
        grid=(1,),
        in_specs=[whole(part.shape) for part in parts],
        out_specs=whole(shape),
        out_shape=jax.ShapeDtypeStruct(shape, parts[0].dtype),
        compiler_params=params(),
    )(*parts)


def scale_kernel(gain_ref, query_ref, key_ref, value_ref, label_ref, own_ref, own_kv_ref):
    gain = gain_ref[...]
    scaled = lambda ref: (ref[...].astype(jnp.float32) * gain).astype(jnp.bfloat16)
    own_ref[...] = scaled(query_ref)
    depth, width = key_ref.shape
    own_kv_ref[:depth, :width] = scaled(key_ref)
    own_kv_ref[:depth, width:] = scaled(value_ref)
    own_kv_ref[depth:, :] = jnp.broadcast_to(label_ref[...], (LABEL_ROWS, 2 * width))


def scale(gain, w_query, w_key, w_value, label):
    depth, width = w_key.shape
    shapes = [w_query.shape, (depth + LABEL_ROWS, 2 * width)]
    return pl.pallas_call(
        scale_kernel,
        grid=(1,),
        in_specs=[whole(a.shape) for a in (gain, w_query, w_key, w_value, label)],
        out_specs=[whole(shape) for shape in shapes],
        out_shape=[jax.ShapeDtypeStruct(shape, jnp.bfloat16) for shape in shapes],
        compiler_params=params(),
    )(gain, w_query, w_key, w_value, label)


def place_kernel(at_ref, from_ref, items_ref, out_ref):
    out_ref[...] = jnp.zeros_like(out_ref)
    for index in range(at_ref.shape[0]):
        at = at_ref[index]

        @pl.when(at >= 0)
        def _():
            out_ref[pl.ds(at, 1)] = items_ref[pl.ds(from_ref[index], 1)]


def place(at, source, items, slots):
    shape = (slots,) + items.shape[1:]
    return pl.pallas_call(
        place_kernel,
        grid_spec=pltpu.PrefetchScalarGridSpec(
            num_scalar_prefetch=2,
            grid=(1,),
            in_specs=[whole(items.shape)],
            out_specs=whole(shape),
        ),
        out_shape=jax.ShapeDtypeStruct(shape, items.dtype),
        compiler_params=params(),
    )(at, source, items)


def assemble(ways_ref, x_refs, held):
    width = x_refs[0].shape[1]
    for index, x_ref in enumerate(x_refs):
        held[:, pl.ds(pl.multiple_of(ways_ref[index] * width, LANE), width)] = x_ref[...]


def columns(held, offsets_ref, units):
    return jnp.concatenate(
        [
            held[:, pl.ds(pl.multiple_of(offsets_ref[unit] * UNIT, LANE), UNIT)]
            for unit in units
        ],
        axis=1,
    )


def rotary(values, cosine, sines):
    return values * cosine + pltpu.roll(values, HD // 2, 1) * sines


def kv_kernel(
    ways_ref, offsets_ref, dest_ref, *refs,
):
    x_refs = refs[:8]
    w_ref, bias_ref, cos_ref, sin_ref, out_ref, pages_ref, factor_ref, label_ref, held = refs[8:]
    step, depth = held.shape
    assemble(ways_ref, x_refs, held)
    squares = jnp.zeros((step, 1), jnp.float32)
    for at in range(0, depth, 1024):
        part = held[:, at : at + 1024].astype(jnp.float32)
        squares += jnp.sum(part * part, axis=-1, keepdims=True)
    factor = lax.rsqrt(squares / depth + EPS)
    factor_ref[...] = factor
    total = jnp.zeros((step, w_ref.shape[1]), jnp.float32)
    span = UNIT + LABEL_ROWS
    for index in range(depth // UNIT):
        total += jnp.dot(
            held[:, pl.ds(pl.multiple_of(offsets_ref[index] * UNIT, LANE), UNIT)],
            w_ref[index * span : index * span + UNIT, :],
            preferred_element_type=jnp.float32,
        )
        label_ref[index : index + 1, :] = w_ref[
            index * span + UNIT : index * span + UNIT + 16, :LANE
        ][:1].astype(jnp.float32)
    total = total * factor + bias_ref[...]
    keyed = rotary(total[:, :HD], cos_ref[...], sin_ref[...]).astype(jnp.bfloat16)
    out_ref[:, :HD] = keyed
    out_ref[:, HD:] = total[:, HD:].astype(jnp.bfloat16)
    block = pl.program_id(0)

    @pl.when(block == 0)
    def _():
        pages_ref[...] = jnp.zeros_like(pages_ref)

    rows = pages_ref.shape[1]
    for page in range(step // rows):
        at = dest_ref[block * (step // rows) + page]
        pages_ref[pl.ds(at, 1)] = out_ref[page * rows : (page + 1) * rows, :][None]


def kv_rows(ways, offsets, dest, xs, w, bias, cosine, sines, slots, page_rows):
    rows, part = xs[0].shape
    step = 256
    by_rows = lambda width: pl.BlockSpec((step, width), lambda i, *_: (i, 0))
    width = w.shape[1]
    depth = part * len(xs)
    pages = (slots, page_rows, width)
    labels = (depth // UNIT, LANE)
    return pl.pallas_call(
        kv_kernel,
        grid_spec=pltpu.PrefetchScalarGridSpec(
            num_scalar_prefetch=3,
            grid=(rows // step,),
            in_specs=[by_rows(part)] * len(xs)
            + [whole(w.shape), whole(bias.shape), by_rows(HD), by_rows(HD)],
            out_specs=[by_rows(width), whole(pages), by_rows(1), whole(labels)],
            scratch_shapes=[pltpu.VMEM((step, depth), jnp.bfloat16)],
        ),
        out_shape=[
            jax.ShapeDtypeStruct((rows, width), jnp.bfloat16),
            jax.ShapeDtypeStruct(pages, jnp.bfloat16),
            jax.ShapeDtypeStruct((rows, 1), jnp.float32),
            jax.ShapeDtypeStruct(labels, jnp.float32),
        ],
        compiler_params=params(),
        cost_estimate=pl.CostEstimate(
            flops=2 * rows * depth * width, bytes_accessed=13_000_000, transcendentals=0
        ),
    )(ways, offsets, dest, *xs, w, bias, cosine, sines)


def query_kernel(units, tail_units, ways_ref, offsets_ref, *refs):
    x_refs, pieces = refs[:8], refs[8:-3]
    out_ref, tail_ref, held = refs[-3:]
    assemble(ways_ref, x_refs, held)
    total = jnp.zeros(out_ref.shape, jnp.float32)
    for piece_ref, own in zip(pieces, units):
        total += jnp.dot(
            columns(held, offsets_ref, own), piece_ref[...], preferred_element_type=jnp.float32
        )
    out_ref[...] = total
    tail_ref[...] = columns(held, offsets_ref, tail_units)


def query_sums(ways, offsets, xs, pieces, units, tail_units):
    rows, part = xs[0].shape
    step = 256
    by_rows = lambda width: pl.BlockSpec((step, width), lambda i, *_: (i, 0))
    width = pieces[0].shape[1]
    depth = part * len(xs)
    tail_width = len(tail_units) * UNIT
    return pl.pallas_call(
        lambda *refs: query_kernel(units, tail_units, *refs),
        grid_spec=pltpu.PrefetchScalarGridSpec(
            num_scalar_prefetch=2,
            grid=(rows // step,),
            in_specs=[by_rows(part)] * len(xs) + [whole(piece.shape) for piece in pieces],
            out_specs=[by_rows(width), by_rows(tail_width)],
            scratch_shapes=[pltpu.VMEM((step, depth), jnp.bfloat16)],
        ),
        out_shape=[
            jax.ShapeDtypeStruct((rows, width), jnp.float32),
            jax.ShapeDtypeStruct((rows, tail_width), jnp.bfloat16),
        ],
        compiler_params=params(),
        cost_estimate=pl.CostEstimate(
            flops=2 * rows * depth * width, bytes_accessed=18_000_000, transcendentals=0
        ),
    )(ways, offsets, *xs, *pieces)


def attend_kernel(
    sums_ref, tail_ref, last_ref, factor_ref, bias_ref, cos_ref, sin_ref, start_ref, kv_ref, out_ref,
):
    step = sums_ref.shape[0]
    block = pl.program_id(0)
    total = sums_ref[...] + jnp.dot(
        tail_ref[...], last_ref[...], preferred_element_type=jnp.float32
    )
    total = total * factor_ref[...] + bias_ref[...]
    heads = total.shape[1] // HD
    query = jnp.concatenate(
        [
            rotary(total[:, h * HD : (h + 1) * HD], cos_ref[...], sin_ref[...]).astype(jnp.bfloat16)
            for h in range(heads)
        ],
        axis=0,
    )
    begin = pl.multiple_of(jnp.maximum(block * step + step - WINDOW, 0), LANE)
    keyed = kv_ref[pl.ds(begin, WINDOW), :HD]
    valued = kv_ref[pl.ds(begin, WINDOW), HD:]
    scores = lax.dot_general(
        query, keyed, (((1,), (1,)), ((), ())), preferred_element_type=jnp.float32
    ) * (HD ** (-0.5))
    key_at = begin + lax.broadcasted_iota(jnp.int32, (step, WINDOW), 1)
    row_at = block * step + lax.broadcasted_iota(jnp.int32, (step, WINDOW), 0)
    allowed = (key_at <= row_at) & (key_at >= start_ref[...])
    for h in range(heads):
        own = jnp.where(allowed, scores[h * step : (h + 1) * step], -1e30)
        raised = jnp.exp(own - jnp.max(own, axis=-1, keepdims=True))
        weights = (raised / jnp.sum(raised, axis=-1, keepdims=True)).astype(jnp.bfloat16)
        mixed = jnp.dot(weights, valued, preferred_element_type=jnp.float32)
        out_ref[:, h * HD : (h + 1) * HD] = mixed.astype(jnp.bfloat16)


def attend(sums, tail, last, factor, bias, cosine, sines, start, kv):
    rows, width = sums.shape
    step = 256
    by_rows = lambda cols: pl.BlockSpec((step, cols), lambda i: (i, 0))
    return pl.pallas_call(
        attend_kernel,
        grid=(rows // step,),
        in_specs=[
            by_rows(width),
            by_rows(tail.shape[1]),
            whole(last.shape),
            by_rows(1),
            whole(bias.shape),
            by_rows(HD),
            by_rows(HD),
            by_rows(1),
            whole(kv.shape),
        ],
        out_specs=by_rows(width),
        out_shape=jax.ShapeDtypeStruct((rows, width), jnp.bfloat16),
        compiler_params=params(),
    )(sums, tail, last, factor, bias, cosine, sines, start, kv)


def after(values, *others):
    return lax.optimization_barrier((tuple(values),) + others)[0]


def body(
    patches, window_order, vis_gain, vis_qkv, vis_qkv_bias, vis_proj, vis_proj_bias, merge_gain,
    img_owner, img_slot, prompt_rows, lang_gain, w_query, b_query, w_key, b_key, w_value, b_value,
    page_owner, page_slot,
):
    phase, rep, tp = lax.axis_index("phase"), lax.axis_index("rep"), lax.axis_index("tp")
    n_phase, n_rep = lax.axis_size("phase"), lax.axis_size("rep")
    groups = n_phase * n_rep
    group = phase * n_rep + rep
    chip, core = tp // 2, tp % 2
    bf16, f32 = jnp.bfloat16, jnp.float32

    up, down = shift("rep", 1), shift("rep", -1)
    fore, back = shift("phase", 1), shift("phase", -1)
    tp_ways = lax.axis_size("tp")
    chips = tp_ways // 2
    across = lambda a, by: lax.ppermute(
        a, "tp", [(i, (i + 2 * by) % tp_ways) for i in range(tp_ways)]
    )
    partner = lambda a: lax.ppermute(a, "tp", [(i, i ^ 1) for i in range(tp_ways)])
    take = lambda a, at: lax.dynamic_index_in_dim(a, at, 0, keepdims=False)

    owner, owners = img_owner[0], page_owner[0]
    label = jnp.concatenate([owner, img_slot[0], owners, page_slot[0]]).astype(bf16)
    label = jnp.pad(label, (0, 2 * w_key.shape[1] - label.shape[0]))[None, :]

    depth = w_query.shape[0]
    gain = lax.dynamic_slice_in_dim(lang_gain, group * depth, depth)[:, None]
    own, own_kv = scale(gain, w_query, w_key, w_value, label)

    kv_all = (own_kv, fore(own_kv), back(own_kv), shift("phase", 2)(own_kv))
    up1, down1 = up(own), down(own)
    x_chips = [prompt_rows] + [across(prompt_rows, by) for by in (1, -1, 2)]

    pages = owners.shape[0]
    rows = prompt_rows.shape[0]
    page_rows = rows // pages
    page_iota = jnp.arange(pages, dtype=jnp.int32)
    first_of = lambda ids: jnp.min(
        jnp.where(ids[..., :, None] == ids[..., None, :], page_iota, pages), axis=-1
    )
    first_page = first_of(owners)
    start = jnp.repeat(first_page, page_rows) * page_rows
    position = jnp.arange(rows, dtype=jnp.int32) - start
    half_dim = HD // 2
    inv_freq = jnp.exp(-jnp.log(1000000.0) * jnp.arange(half_dim).astype(f32) / half_dim)
    angles = position.astype(f32)[:, None] * inv_freq[None, :]
    cosine, sines = jnp.cos(angles), jnp.sin(angles)
    cosine = jnp.concatenate([cosine, cosine], axis=1)
    sines = jnp.concatenate([-sines, sines], axis=1)
    patch_count, width = patches.shape
    merge = 4
    order = window_order[0].reshape(patch_count // merge, merge).T[:, :, None]
    chunks = vis_qkv.shape[1] // VHD
    bias_pad = jnp.pad(vis_qkv_bias.reshape(chunks, VHD), ((0, 0), (0, LANE - VHD))).reshape(1, -1)
    order, bias_pad, cosine, sines, up1, down1, *kv_all = after(
        (order, bias_pad, cosine, sines, up1, down1, *kv_all)
    )

    kv_weights = lax.all_gather(join(*kv_all), "rep", axis=0, tiled=True)
    up2, down2 = up(up1), down(down1)
    near = join(own, up1, down1)
    near_fore, near_back = fore(near), back(near)
    keep, send, resid = vision_partial(
        order, patches, vis_gain[None, :], vis_qkv, bias_pad, vis_proj, jnp.stack([core, chip])
    )
    keep, send, up2, down2 = after((keep, send, up2, down2))

    up3, down3 = up(up2), down(down2)
    chip_sum = (keep.astype(f32) + partner(send).astype(f32)).astype(bf16)
    chip_sum, up3, down3, near_fore, near_back = after(
        (chip_sum, up3, down3, near_fore, near_back)
    )

    up4 = up(up3)
    near_two = fore(near_fore)
    arrived = [across(take(chip_sum, (chip + by) % chips), by) for by in (1, -1, 2)]
    far = join(up2, down2, up3, down3, up4)
    far_fore, far_back = fore(far), back(far)
    x_chips = list(after((*x_chips, up4)))[:4]
    xs = x_chips + [partner(a) for a in x_chips]

    half = width // 2
    cols = lambda a: lax.dynamic_slice_in_dim(a, core * half, half, a.ndim - 1)
    mixed = resid.astype(f32) + cols(vis_proj_bias)
    for part in [take(chip_sum, chip)] + arrived:
        mixed = mixed + part.astype(f32)
    squares = jnp.sum(mixed * mixed, axis=-1).reshape(2, -1)
    squares = squares + partner(squares)
    factor = lax.rsqrt(squares.reshape(-1, 1) / width + EPS)
    merged = (mixed * factor * cols(merge_gain)).astype(bf16)
    requests = owner.shape[0]
    merged = merged.reshape(requests, -1, half)
    outgoing = place(owner, jnp.arange(requests, dtype=jnp.int32), merged, groups)
    images = lax.all_to_all(outgoing, ("phase", "rep"), split_axis=0, concat_axis=0, tiled=True)

    ways = jnp.stack(
        [((chip - by) % chips) * 2 + side for side in (core, 1 - core) for by in (0, 1, -1, 2)]
    ).astype(jnp.int32)
    hops = (0, -1, 1, 2)
    offset_of = lambda dp, at: ((phase + dp) % n_phase) * n_rep + at % n_rep
    kv_offsets = jnp.stack([offset_of(dp, at) for at in range(n_rep) for dp in hops])
    kv, outgoing_pages, row_factor, labels = kv_rows(
        ways, kv_offsets.astype(jnp.int32), owners * CAP + page_iota - first_page, xs, kv_weights,
        jnp.concatenate([b_key, b_value])[None, :], cosine, sines, n_rep * CAP, page_rows,
    )
    arrived_pages = lax.all_to_all(
        outgoing_pages.reshape(n_rep, CAP, page_rows, -1), "rep", split_axis=0, concat_axis=0, tiled=True
    )

    labels = labels[:, : 4 * requests].astype(jnp.int32).reshape(n_rep, n_phase, 4, -1)
    image_at = jnp.sum(
        jnp.where(labels[:, :, 0] == group, labels[:, :, 1] + 1, 0), axis=-1
    ).reshape(-1) - 1
    page_at = jnp.where(labels[:, 0, 2] == rep, labels[:, 0, 3], -1).reshape(-1)
    page_from = (
        jnp.arange(n_rep, dtype=jnp.int32)[:, None] * CAP + page_iota - first_of(labels[:, 0, 2])
    ).reshape(-1)
    image_buffer = place(image_at, kv_offsets.astype(jnp.int32), images, groups).reshape(-1, half)
    kv_pool = place(page_at, page_from, arrived_pages.reshape(n_rep * CAP, page_rows, -1), pages)

    far_fore, far_back, near_two = after((far_fore, far_back, near_two))
    far_two = back(far_back)
    offsets, pieces, units = [], [], []

    def units_of(dp, drs):
        at = len(offsets)
        offsets.extend(offset_of(dp, rep + dr) for dr in drs)
        return list(range(at, at + len(drs)))

    near_reps, far_reps = (0, -1, 1), (-2, 2, -3, 3, -4)
    for piece, dp, reps in (
        (near, 0, near_reps), (near_fore, -1, near_reps), (near_back, 1, near_reps),
        (near_two, 2, near_reps), (far, 0, far_reps), (far_fore, -1, far_reps),
        (far_back, 1, far_reps),
    ):
        pieces.append(piece)
        units.append(units_of(dp, reps))
    last = units_of(2, far_reps)
    sums, tail = query_sums(ways, jnp.stack(offsets).astype(jnp.int32), xs, pieces, units, last)
    attn_out = attend(
        sums, tail, far_two, row_factor, b_query[None, :], cosine, sines, start[:, None], kv
    )
    return (image_buffer, attn_out, kv_pool)


def solution(mesh):
    split, cut = P(("phase", "rep"), None), P(("phase", "rep"), "tp")
    return jax.shard_map(
        body,
        mesh=mesh,
        in_specs=(
            split, split, P(), P(None, "tp"), P("tp"), P("tp", None), P(), P(), split, split,
            cut, P(), cut, P("tp"), cut, P("tp"), cut, P("tp"), split, split,
        ),
        out_specs=(cut, cut, P(("phase", "rep"), None, "tp")),
        check_vma=False,
    )
```

profile of v0, /device:TPU:2, one launch (start us, length us, event | category | flops | bytes accessed | tf_op | source)
XLA Modules:
  0.0 256.9 jit_solution(7656274241788632843)
XLA Ops:
  10.8 1.9 shard_map.211
  12.7 3.2 %collective-permute-start.7 = (bf16[272,256]{1,0:T(8,128)(2,1)}, bf16[272,256]{1,0:T(8,128)(2,1)S(1)}, u32[]{:S(2)}, u32[]{:S(2)}) collective-permute-start(bf16[272,256]{1,0:T(8,128)(2,1)} %get-tuple-element.57.refs_0_), channel_id=1, source_target_pairs={{0,128},{64,192},{128,0},{192,64},{1,129},{65,193},{129,1},{193,65... | collective-permute-start | bytes 417800 | tf_op jit(solution)/shard_map/ppermute | solution.py:30
  15.9 1.1 collective-permute-start.6
  16.9 1.0 collective-permute-start.5
  17.9 5.9 %collective-permute-start.4 = (bf16[256,512]{1,0:T(8,128)(2,1)}, bf16[256,512]{1,0:T(8,128)(2,1)S(1)}, u32[]{:S(2)}, u32[]{:S(2)}) collective-permute-start(bf16[256,512]{1,0:T(8,128)(2,1)} %get-tuple-element.40.refs_0_), channel_id=1, source_target_pairs={{0,56},{8,0},{16,8},{24,16},{32,24},{40,32},{48,40},{56,48},{1,57}... | collective-permute-start | bytes 786440 | tf_op jit(solution)/shard_map/ppermute | solution.py:30
  23.8 0.9 select_reduce_fusion.1
  24.7 1.2 broadcast_multiply_fusion
  26.0 1.0 fusion.3
  29.1 1.0 pad_maximum_fusion
  30.2 1.9 collective-permute-done.3.refs_1_
  32.1 2.1 shard_map.214
  34.9 1.5 copy.36.w_ref
  37.1 3.2 %collective-permute-start.9 = (bf16[256,512]{1,0:T(8,128)(2,1)S(1)}, bf16[256,512]{1,0:T(8,128)(2,1)S(1)}, u32[]{:S(2)}, u32[]{:S(2)}) collective-permute-start(bf16[256,512]{1,0:T(8,128)(2,1)S(1)} %collective-permute-done.4.refs_2_), channel_id=1, source_target_pairs={{0,56},{8,0},{16,8},{24,16},{32,24},{40,32},{48,40},{56,48},{1,57}... | collective-permute-start | bytes 786440 | tf_op jit(solution)/shard_map/ppermute | solution.py:30
  40.3 1.0 copy.35.order_ref
  41.3 16.0 %shard_map.212 = (bf16[4,256,640]{2,1,0:T(8,128)(2,1)}, bf16[4,256,640]{2,1,0:T(8,128)(2,1)}, bf16[256,640]{1,0:T(8,128)(2,1)}) custom-call(s32[2]{0:T(128)} %pad_add_fusion.own_ref, s32[4,256,1]{2,1,0:T(8,128)} %copy.35.order_ref, bf16[1024,1280]{1,0:T(8,128)(2,1)} %patches_ref.1, f32[1,1280]{1,0:T(1,128)} %broadcast_in_dim.58.gain_ref, ...), custom_call_target="tpu_custom_call" | custom-call | flops 10000000000 | bytes 8000000 | tf_op jit(solution)/shard_map/pallas_call | solution.py:116
  57.5 2.3 shard_map.213.refs_10_
  59.8 2.3 collective-permute-start.14
  62.7 3.2 %collective-permute-start.12 = (bf16[256,512]{1,0:T(8,128)(2,1)S(1)}, bf16[256,512]{1,0:T(8,128)(2,1)S(1)}, u32[]{:S(2)}, u32[]{:S(2)}) collective-permute-start(bf16[256,512]{1,0:T(8,128)(2,1)S(1)} %collective-permute-done.9.refs_1_), channel_id=1, source_target_pairs={{0,56},{8,0},{16,8},{24,16},{32,24},{40,32},{48,40},{56,48},{1,57}... | collective-permute-start | bytes 786440 | tf_op jit(solution)/shard_map/ppermute | solution.py:30
  66.3 12.0 %collective-permute-done.11.refs_2_ = bf16[256,512]{1,0:T(8,128)(2,1)S(1)} collective-permute-done((bf16[256,512]{1,0:T(8,128)(2,1)S(1)}, bf16[256,512]{1,0:T(8,128)(2,1)S(1)}, u32[]{:S(2)}, u32[]{:S(2)}) %collective-permute-start.11) | collective-permute-done | bytes 262176 | tf_op jit(solution)/shard_map/ppermute | solution.py:30
  78.2 1.5 collective-permute-done.14.refs_12_
  79.7 3.2 %collective-permute-done.13.refs_11_ = bf16[768,512]{1,0:T(8,128)(2,1)S(1)} collective-permute-done((bf16[768,512]{1,0:T(8,128)(2,1)}, bf16[768,512]{1,0:T(8,128)(2,1)S(1)}, u32[]{:S(2)}, u32[]{:S(2)}) %collective-permute-start.13) | collective-permute-done | bytes 786464 | tf_op jit(solution)/shard_map/ppermute | solution.py:30
  82.9 15.4 %collective-permute-done.15.refs_4_ = bf16[256,512]{1,0:T(8,128)(2,1)S(1)} collective-permute-done((bf16[256,512]{1,0:T(8,128)(2,1)S(1)}, bf16[256,512]{1,0:T(8,128)(2,1)S(1)}, u32[]{:S(2)}, u32[]{:S(2)}) %collective-permute-start.15) | collective-permute-done | bytes 262176 | tf_op jit(solution)/shard_map/ppermute | solution.py:30
  99.0 2.4 shard_map.218.refs_14_
  102.8 1.5 collective-permute-start.20
  104.3 1.2 collective-permute-start
  105.5 1.4 collective-permute-start.2
  106.9 2.1 collective-permute-start.22
  109.0 4.4 %collective-permute-done.20 = bf16[256,640]{1,0:T(8,128)(2,1)S(1)} collective-permute-done((bf16[256,640]{1,0:T(8,128)(2,1)S(1)}, bf16[256,640]{1,0:T(8,128)(2,1)S(1)}, u32[]{:S(2)}, u32[]{:S(2)}) %collective-permute-start.20) | collective-permute-done | bytes 327712 | tf_op jit(solution)/shard_map/ppermute | solution.py:421
  113.5 1.6 collective-permute-start.26
  115.0 22.3 %collective-permute-done.22 = bf16[256,640]{1,0:T(8,128)(2,1)} collective-permute-done((bf16[256,640]{1,0:T(8,128)(2,1)S(1)}, bf16[256,640]{1,0:T(8,128)(2,1)}, u32[]{:S(2)}, u32[]{:S(2)}) %collective-permute-start.22) | collective-permute-done | bytes 327712 | tf_op jit(solution)/shard_map/ppermute | solution.py:421
  137.3 28.4 %collective-permute-start.21 = (bf16[256,640]{1,0:T(8,128)(2,1)}, bf16[256,640]{1,0:T(8,128)(2,1)}, u32[]{:S(2)}, u32[]{:S(2)}) collective-permute-start(bf16[256,640]{1,0:T(8,128)(2,1)} %get-tuple-element.79), channel_id=1, source_target_pairs={{0,6},{1,7},{2,0},{3,1},{4,2},{5,3},{6,4},{7,5},{8,14},{9,15},{10,... | collective-permute-start | bytes 983048 | tf_op jit(solution)/shard_map/ppermute | solution.py:421
  165.8 4.9 %collective-permute-done.21 = bf16[256,640]{1,0:T(8,128)(2,1)} collective-permute-done((bf16[256,640]{1,0:T(8,128)(2,1)}, bf16[256,640]{1,0:T(8,128)(2,1)}, u32[]{:S(2)}, u32[]{:S(2)}) %collective-permute-start.21) | collective-permute-done | bytes 327712 | tf_op jit(solution)/shard_map/ppermute | solution.py:421
  170.7 1.2 collective-permute-start.24
  171.9 1.4 multiply_reduce_fusion
  175.2 2.1 multiply_convert_fusion
  177.8 2.7 %shard_map.216 = bf16[32,16,640]{2,1,0:T(8,128)(2,1)} custom-call(s32[16]{0:T(128)} %bitcast.137, s32[16]{0:T(128)} %iota.29.from_ref, bf16[16,16,640]{2,1,0:T(8,128)(2,1)} %bitcast.124), custom_call_target="tpu_custom_call" | custom-call | tf_op jit(solution)/shard_map/pallas_call | solution.py:199
  180.5 5.2 %all-to-all-start = ((bf16[32,16,640]{2,1,0:T(8,128)(2,1)}), bf16[32,16,640]{2,1,0:T(8,128)(2,1)S(1)}, u32[]{:S(2)}, u32[]{:S(2)}) async-start(bf16[32,16,640]{2,1,0:T(8,128)(2,1)} %shard_map.216), calls=%async_computation | async-start | bytes 1310720 | tf_op jit(solution)/shard_map/all_to_all | solution.py:499
  185.9 1.0 mul.95.start_ref
  189.4 16.8 %collective-permute-done.24.refs_15_ = bf16[1280,512]{1,0:T(8,128)(2,1)} collective-permute-done((bf16[1280,512]{1,0:T(8,128)(2,1)S(1)}, bf16[1280,512]{1,0:T(8,128)(2,1)}, u32[]{:S(2)}, u32[]{:S(2)}) %collective-permute-start.24) | collective-permute-done | bytes 1310752 | tf_op jit(solution)/shard_map/ppermute | solution.py:30
  206.1 10.9 %shard_map.219 = (f32[512,512]{1,0:T(8,128)}, bf16[512,1280]{1,0:T(8,128)(2,1)}) custom-call(s32[8]{0:T(128)} %stack.242.ways_ref.refs_0_, s32[32]{0:T(128)} %stack.311.refs_1_, bf16[512,1024]{1,0:T(8,128)(2,1)} %refs_2_, bf16[512,1024]{1,0:T(8,128)(2,1)} %collective-permute-done.refs_1_.refs_3_, bf16[512,1024]{1,0:T(8,128)(2,1)} %collective-permute-done.1.refs_2_.refs_4_, ...), custom_call_target="tpu_custom_call" | custom-call | flops 4294967296 | bytes 18000000 | tf_op jit(solution)/shard_map/pallas_call | solution.py:323
  217.1 10.3 %shard_map.215 = (bf16[512,256]{1,0:T(8,128)(2,1)}, bf16[40,32,256]{2,1,0:T(8,128)(2,1)}, f32[512,1]{1,0:T(8,128)}, f32[32,128]{1,0:T(8,128)}) custom-call(s32[8]{0:T(128)} %stack.242.ways_ref.refs_0_, s32[32]{0:T(128)} %stack.275.offsets_ref.from_ref, s32[16]{0:T(128)} %get-tuple-element.86.dest_ref, bf16[512,1024]{1,0:T(8,128)(2,1)} %refs_2_, ...), custom_call_target="tpu_custom_call" | custom-call | flops 2147483648 | bytes 13000000 | tf_op jit(solution)/shard_map/pallas_call | solution.py:280
  227.4 3.6 %all-to-all-start.1 = ((bf16[8,5,32,256]{3,2,1,0:T(8,128)(2,1)}), bf16[8,5,32,256]{3,2,1,0:T(8,128)(2,1)S(1)}, u32[]{:S(2)}, u32[]{:S(2)}) async-start(bf16[8,5,32,256]{3,2,1,0:T(8,128)(2,1)} %bitcast.125), calls=%async_computation.1 | async-start | bytes 1310720 | tf_op jit(solution)/shard_map/all_to_all | solution.py:511
  233.9 2.9 %shard_map.217 = bf16[32,16,640]{2,1,0:T(8,128)(2,1)} custom-call(s32[32]{0:T(128)} %sub.50.at_ref, s32[32]{0:T(128)} %stack.275.offsets_ref.from_ref, bf16[32,16,640]{2,1,0:T(8,128)(2,1)} %copy-done), custom_call_target="tpu_custom_call" | custom-call | tf_op jit(solution)/shard_map/pallas_call | solution.py:199
  236.8 1.1 copy-done.2
  237.9 5.8 %shard_map.220 = bf16[512,512]{1,0:T(8,128)(2,1)} custom-call(f32[512,512]{1,0:T(8,128)} %get-tuple-element.72.sums_ref, bf16[512,1280]{1,0:T(8,128)(2,1)} %get-tuple-element.73.tail_ref, bf16[1280,512]{1,0:T(8,128)(2,1)} %copy-done.2, f32[512,1]{1,0:T(8,128)} %get-tuple-element.74.factor_ref, f32[1,512]{1,0:T(1,128)} %bitcast.136, ...), custom_call_target="tpu_custom_call" | custom-call | tf_op jit(solution)/shard_map/pallas_call | solution.py:381
  243.8 1.8 all-to-all-done.1
  245.6 0.9 copy-done.1
  246.4 3.6 %shard_map.221 = bf16[16,32,256]{2,1,0:T(8,128)(2,1)} custom-call(s32[128]{0:T(128)} %select_n.328.at_ref, s32[128]{0:T(128)} %sub.52.from_ref, bf16[40,32,256]{2,1,0:T(8,128)(2,1)} %bitcast.123), custom_call_target="tpu_custom_call" | custom-call | tf_op jit(solution)/shard_map/pallas_call | solution.py:199
  (130 shorter events, 18.2 us)
Async XLA Ops:
  7.2 19.9 %copy-start.20 = (f32[480]{0:T(512)S(1)}, f32[480]{0:T(512)}, u32[]{:S(2)}) copy-start(f32[480]{0:T(512)} %param.24) | copy-start | bytes 5764
  7.2 21.1 %copy-start.19 = (s32[1,1024]{1,0:T(1,128)S(1)}, s32[1,1024]{1,0:T(1,128)}, u32[]{:S(2)}) copy-start(s32[1,1024]{1,0:T(1,128)} %param.21) | copy-start | bytes 12292
  7.2 209.9 %all-gather.2.cloned.1.call-start = ((), (), s32[]{:S(2)}) async-start(), calls=%async_computation.2 | async-start | bytes 5013504 | tf_op jit(solution)/shard_map/all_gather | solution.py:464
  12.7 17.5 %collective-permute-start.7 = (bf16[272,256]{1,0:T(8,128)(2,1)}, bf16[272,256]{1,0:T(8,128)(2,1)S(1)}, u32[]{:S(2)}, u32[]{:S(2)}) collective-permute-start(bf16[272,256]{1,0:T(8,128)(2,1)} %get-tuple-element.57.refs_0_), channel_id=1, source_target_pairs={{0,128},{64,192},{128,0},{192,64},{1,129},{65,193},{129,1},{193,65... | collective-permute-start | bytes 417800 | tf_op jit(solution)/shard_map/ppermute | solution.py:30
  15.9 14.3 %collective-permute-start.6 = (bf16[272,256]{1,0:T(8,128)(2,1)}, bf16[272,256]{1,0:T(8,128)(2,1)S(1)}, u32[]{:S(2)}, u32[]{:S(2)}) collective-permute-start(bf16[272,256]{1,0:T(8,128)(2,1)} %get-tuple-element.57.refs_0_), channel_id=1, source_target_pairs={{0,192},{64,0},{128,64},{192,128},{1,193},{65,1},{129,65},{193,129... | collective-permute-start | bytes 417800 | tf_op jit(solution)/shard_map/ppermute | solution.py:30
  16.9 13.2 %collective-permute-start.5 = (bf16[272,256]{1,0:T(8,128)(2,1)}, bf16[272,256]{1,0:T(8,128)(2,1)S(1)}, u32[]{:S(2)}, u32[]{:S(2)}) collective-permute-start(bf16[272,256]{1,0:T(8,128)(2,1)} %get-tuple-element.57.refs_0_), channel_id=1, source_target_pairs={{0,64},{64,128},{128,192},{192,0},{1,65},{65,129},{129,193},{193,1... | collective-permute-start | bytes 417800 | tf_op jit(solution)/shard_map/ppermute | solution.py:30
  17.9 12.3 %collective-permute-start.4 = (bf16[256,512]{1,0:T(8,128)(2,1)}, bf16[256,512]{1,0:T(8,128)(2,1)S(1)}, u32[]{:S(2)}, u32[]{:S(2)}) collective-permute-start(bf16[256,512]{1,0:T(8,128)(2,1)} %get-tuple-element.40.refs_0_), channel_id=1, source_target_pairs={{0,56},{8,0},{16,8},{24,16},{32,24},{40,32},{48,40},{56,48},{1,57}... | collective-permute-start | bytes 786440 | tf_op jit(solution)/shard_map/ppermute | solution.py:30
  23.8 8.3 %collective-permute-start.3 = (bf16[256,512]{1,0:T(8,128)(2,1)}, bf16[256,512]{1,0:T(8,128)(2,1)S(1)}, u32[]{:S(2)}, u32[]{:S(2)}) collective-permute-start(bf16[256,512]{1,0:T(8,128)(2,1)} %get-tuple-element.40.refs_0_), channel_id=1, source_target_pairs={{0,8},{8,16},{16,24},{24,32},{32,40},{40,48},{48,56},{56,0},{1,9},... | collective-permute-start | bytes 786440 | tf_op jit(solution)/shard_map/ppermute | solution.py:30
  30.2 6.9 %copy-start.12 = (bf16[256,512]{1,0:T(8,128)(2,1)}, bf16[256,512]{1,0:T(8,128)(2,1)S(1)}, u32[]{:S(2)}) copy-start(bf16[256,512]{1,0:T(8,128)(2,1)S(1)} %collective-permute-done.4.refs_2_) | copy-start | bytes 786436
  37.0 20.3 %collective-permute-start.8 = (bf16[256,512]{1,0:T(8,128)(2,1)S(1)}, bf16[256,512]{1,0:T(8,128)(2,1)S(1)}, u32[]{:S(2)}, u32[]{:S(2)}) collective-permute-start(bf16[256,512]{1,0:T(8,128)(2,1)S(1)} %collective-permute-done.3.refs_1_), channel_id=1, source_target_pairs={{0,8},{8,16},{16,24},{24,32},{32,40},{40,48},{48,56},{56,0},{1,9},... | collective-permute-start | bytes 786440 | tf_op jit(solution)/shard_map/ppermute | solution.py:30
  37.1 20.3 %collective-permute-start.9 = (bf16[256,512]{1,0:T(8,128)(2,1)S(1)}, bf16[256,512]{1,0:T(8,128)(2,1)S(1)}, u32[]{:S(2)}, u32[]{:S(2)}) collective-permute-start(bf16[256,512]{1,0:T(8,128)(2,1)S(1)} %collective-permute-done.4.refs_2_), channel_id=1, source_target_pairs={{0,56},{8,0},{16,8},{24,16},{32,24},{40,32},{48,40},{56,48},{1,57}... | collective-permute-start | bytes 786440 | tf_op jit(solution)/shard_map/ppermute | solution.py:30
  57.3 8.6 %copy-start.4 = (bf16[4,256,640]{2,1,0:T(8,128)(2,1)S(1)}, bf16[4,256,640]{2,1,0:T(8,128)(2,1)}, u32[]{:S(2)}) copy-start(bf16[4,256,640]{2,1,0:T(8,128)(2,1)} %get-tuple-element.48) | copy-start | bytes 3932164
  57.4 8.9 %copy-start.7 = (bf16[256,512]{1,0:T(8,128)(2,1)}, bf16[256,512]{1,0:T(8,128)(2,1)S(1)}, u32[]{:S(2)}) copy-start(bf16[256,512]{1,0:T(8,128)(2,1)S(1)} %collective-permute-done.8.refs_0_) | copy-start | bytes 786436
  57.4 8.9 %copy-start.8 = (bf16[256,512]{1,0:T(8,128)(2,1)}, bf16[256,512]{1,0:T(8,128)(2,1)S(1)}, u32[]{:S(2)}) copy-start(bf16[256,512]{1,0:T(8,128)(2,1)S(1)} %collective-permute-done.9.refs_1_) | copy-start | bytes 786436
  57.4 5.3 %collective-permute-start.10 = (bf16[4,256,640]{2,1,0:T(8,128)(2,1)}, bf16[4,256,640]{2,1,0:T(8,128)(2,1)S(1)}, u32[]{:S(2)}, u32[]{:S(2)}) collective-permute-start(bf16[4,256,640]{2,1,0:T(8,128)(2,1)} %get-tuple-element.49), channel_id=1, source_target_pairs={{0,1},{1,0},{2,3},{3,2},{4,5},{5,4},{6,7},{7,6},{8,9},{9,8},{10,11... | collective-permute-start | bytes 3932168 | tf_op jit(solution)/shard_map/ppermute | solution.py:424
  59.8 19.9 %collective-permute-start.14 = (bf16[768,512]{1,0:T(8,128)(2,1)}, bf16[768,512]{1,0:T(8,128)(2,1)S(1)}, u32[]{:S(2)}, u32[]{:S(2)}) collective-permute-start(bf16[768,512]{1,0:T(8,128)(2,1)} %shard_map.213.refs_10_), channel_id=1, source_target_pairs={{0,192},{64,0},{128,64},{192,128},{1,193},{65,1},{129,65},{193,129... | collective-permute-start | bytes 2359304 | tf_op jit(solution)/shard_map/ppermute | solution.py:30
  62.1 20.8 %collective-permute-start.13 = (bf16[768,512]{1,0:T(8,128)(2,1)}, bf16[768,512]{1,0:T(8,128)(2,1)S(1)}, u32[]{:S(2)}, u32[]{:S(2)}) collective-permute-start(bf16[768,512]{1,0:T(8,128)(2,1)} %shard_map.213.refs_10_), channel_id=1, source_target_pairs={{0,64},{64,128},{128,192},{192,0},{1,65},{65,129},{129,193},{193,1... | collective-permute-start | bytes 2359304 | tf_op jit(solution)/shard_map/ppermute | solution.py:30
  62.1 44.8 %collective-permute-start.1 = (bf16[512,1024]{1,0:T(8,128)(2,1)}, bf16[512,1024]{1,0:T(8,128)(2,1)}, u32[]{:S(2)}, u32[]{:S(2)}) collective-permute-start(bf16[512,1024]{1,0:T(8,128)(2,1)} %refs_2_), channel_id=1, source_target_pairs={{0,6},{1,7},{2,0},{3,1},{4,2},{5,3},{6,4},{7,5},{8,14},{9,15},{10,... | collective-permute-start | bytes 3145736 | tf_op jit(solution)/shard_map/ppermute | solution.py:421
  62.7 15.5 %collective-permute-start.11 = (bf16[256,512]{1,0:T(8,128)(2,1)S(1)}, bf16[256,512]{1,0:T(8,128)(2,1)S(1)}, u32[]{:S(2)}, u32[]{:S(2)}) collective-permute-start(bf16[256,512]{1,0:T(8,128)(2,1)S(1)} %collective-permute-done.8.refs_0_), channel_id=1, source_target_pairs={{0,8},{8,16},{16,24},{24,32},{32,40},{40,48},{48,56},{56,0},{1,9},... | collective-permute-start | bytes 786440 | tf_op jit(solution)/shard_map/ppermute | solution.py:30
  62.7 15.5 %collective-permute-start.12 = (bf16[256,512]{1,0:T(8,128)(2,1)S(1)}, bf16[256,512]{1,0:T(8,128)(2,1)S(1)}, u32[]{:S(2)}, u32[]{:S(2)}) collective-permute-start(bf16[256,512]{1,0:T(8,128)(2,1)S(1)} %collective-permute-done.9.refs_1_), channel_id=1, source_target_pairs={{0,56},{8,0},{16,8},{24,16},{32,24},{40,32},{48,40},{56,48},{1,57}... | collective-permute-start | bytes 786440 | tf_op jit(solution)/shard_map/ppermute | solution.py:30
  78.2 20.1 %copy-start.9 = (bf16[256,512]{1,0:T(8,128)(2,1)}, bf16[256,512]{1,0:T(8,128)(2,1)S(1)}, u32[]{:S(2)}) copy-start(bf16[256,512]{1,0:T(8,128)(2,1)S(1)} %collective-permute-done.11.refs_2_) | copy-start | bytes 786436
  78.2 20.1 %copy-start.10 = (bf16[256,512]{1,0:T(8,128)(2,1)}, bf16[256,512]{1,0:T(8,128)(2,1)S(1)}, u32[]{:S(2)}) copy-start(bf16[256,512]{1,0:T(8,128)(2,1)S(1)} %collective-permute-done.12.refs_3_) | copy-start | bytes 786436
  79.7 21.8 %copy-start.25 = (bf16[768,512]{1,0:T(8,128)(2,1)}, bf16[768,512]{1,0:T(8,128)(2,1)S(1)}, u32[]{:S(2)}) copy-start(bf16[768,512]{1,0:T(8,128)(2,1)S(1)} %collective-permute-done.14.refs_12_) | copy-start | bytes 2359300
  82.9 18.5 %copy-start.26 = (bf16[768,512]{1,0:T(8,128)(2,1)}, bf16[768,512]{1,0:T(8,128)(2,1)S(1)}, u32[]{:S(2)}) copy-start(bf16[768,512]{1,0:T(8,128)(2,1)S(1)} %collective-permute-done.13.refs_11_) | copy-start | bytes 2359300
  82.9 15.4 %collective-permute-start.15 = (bf16[256,512]{1,0:T(8,128)(2,1)S(1)}, bf16[256,512]{1,0:T(8,128)(2,1)S(1)}, u32[]{:S(2)}, u32[]{:S(2)}) collective-permute-start(bf16[256,512]{1,0:T(8,128)(2,1)S(1)} %collective-permute-done.11.refs_2_), channel_id=1, source_target_pairs={{0,8},{8,16},{16,24},{24,32},{32,40},{40,48},{48,56},{56,0},{1,9},... | collective-permute-start | bytes 786440 | tf_op jit(solution)/shard_map/ppermute | solution.py:30
  101.4 64.3 %copy-start.21 = (f32[1280]{0:T(1024)S(1)}, f32[1280]{0:T(1024)}, u32[]{:S(2)}) copy-start(f32[1280]{0:T(1024)} %param.26) | copy-start | bytes 15364
  101.4 69.3 %copy-start.3 = (bf16[1280,512]{1,0:T(8,128)(2,1)S(1)}, bf16[1280,512]{1,0:T(8,128)(2,1)}, u32[]{:S(2)}) copy-start(bf16[1280,512]{1,0:T(8,128)(2,1)} %shard_map.218.refs_14_) | copy-start | bytes 3932164
  101.5 70.4 %copy-start.5 = (bf16[256,640]{1,0:T(8,128)(2,1)S(1)}, bf16[256,640]{1,0:T(8,128)(2,1)}, u32[]{:S(2)}) copy-start(bf16[256,640]{1,0:T(8,128)(2,1)} %get-tuple-element.64) | copy-start | bytes 983044
  101.5 73.5 %collective-permute-start.25 = (bf16[1280,512]{1,0:T(8,128)(2,1)}, bf16[1280,512]{1,0:T(8,128)(2,1)}, u32[]{:S(2)}, u32[]{:S(2)}) collective-permute-start(bf16[1280,512]{1,0:T(8,128)(2,1)} %shard_map.218.refs_14_), channel_id=1, source_target_pairs={{0,192},{64,0},{128,64},{192,128},{1,193},{65,1},{129,65},{193,129... | collective-permute-start | bytes 3932168 | tf_op jit(solution)/shard_map/ppermute | solution.py:30
  102.8 70.6 %copy-start.22 = (f32[1280]{0:T(1024)S(1)}, f32[1280]{0:T(1024)}, u32[]{:S(2)}) copy-start(f32[1280]{0:T(1024)} %param.27) | copy-start | bytes 15364
  102.8 10.6 %collective-permute-start.20 = (bf16[256,640]{1,0:T(8,128)(2,1)S(1)}, bf16[256,640]{1,0:T(8,128)(2,1)S(1)}, u32[]{:S(2)}, u32[]{:S(2)}) collective-permute-start(bf16[256,640]{1,0:T(8,128)(2,1)S(1)} %get-tuple-element.77), channel_id=1, source_target_pairs={{0,2},{1,3},{2,4},{3,5},{4,6},{5,7},{6,0},{7,1},{8,10},{9,11},{10,... | collective-permute-start | bytes 983048 | tf_op jit(solution)/shard_map/ppermute | solution.py:421
  104.3 69.0 %collective-permute-start = (bf16[512,1024]{1,0:T(8,128)(2,1)}, bf16[512,1024]{1,0:T(8,128)(2,1)}, u32[]{:S(2)}, u32[]{:S(2)}) collective-permute-start(bf16[512,1024]{1,0:T(8,128)(2,1)} %refs_2_), channel_id=1, source_target_pairs={{0,2},{1,3},{2,4},{3,5},{4,6},{5,7},{6,0},{7,1},{8,10},{9,11},{10,... | collective-permute-start | bytes 3145736 | tf_op jit(solution)/shard_map/ppermute | solution.py:421
  105.5 68.0 %collective-permute-start.2 = (bf16[512,1024]{1,0:T(8,128)(2,1)}, bf16[512,1024]{1,0:T(8,128)(2,1)}, u32[]{:S(2)}, u32[]{:S(2)}) collective-permute-start(bf16[512,1024]{1,0:T(8,128)(2,1)} %refs_2_), channel_id=1, source_target_pairs={{0,4},{1,5},{2,6},{3,7},{4,0},{5,1},{6,2},{7,3},{8,12},{9,13},{10,... | collective-permute-start | bytes 3145736 | tf_op jit(solution)/shard_map/ppermute | solution.py:421
  106.9 30.4 %collective-permute-start.22 = (bf16[256,640]{1,0:T(8,128)(2,1)S(1)}, bf16[256,640]{1,0:T(8,128)(2,1)}, u32[]{:S(2)}, u32[]{:S(2)}) collective-permute-start(bf16[256,640]{1,0:T(8,128)(2,1)S(1)} %get-tuple-element.78), channel_id=1, source_target_pairs={{0,4},{1,5},{2,6},{3,7},{4,0},{5,1},{6,2},{7,3},{8,12},{9,13},{10,... | collective-permute-start | bytes 983048 | tf_op jit(solution)/shard_map/ppermute | solution.py:421
  113.5 61.2 %collective-permute-start.26 = (bf16[768,512]{1,0:T(8,128)(2,1)}, bf16[768,512]{1,0:T(8,128)(2,1)}, u32[]{:S(2)}, u32[]{:S(2)}) collective-permute-start(bf16[768,512]{1,0:T(8,128)(2,1)} %copy-done.26), channel_id=1, source_target_pairs={{0,64},{64,128},{128,192},{192,0},{1,65},{65,129},{129,193},{193,1... | collective-permute-start | bytes 2359304 | tf_op jit(solution)/shard_map/ppermute | solution.py:30
  137.3 33.4 %collective-permute-start.21 = (bf16[256,640]{1,0:T(8,128)(2,1)}, bf16[256,640]{1,0:T(8,128)(2,1)}, u32[]{:S(2)}, u32[]{:S(2)}) collective-permute-start(bf16[256,640]{1,0:T(8,128)(2,1)} %get-tuple-element.79), channel_id=1, source_target_pairs={{0,6},{1,7},{2,0},{3,1},{4,2},{5,3},{6,4},{7,5},{8,14},{9,15},{10,... | collective-permute-start | bytes 983048 | tf_op jit(solution)/shard_map/ppermute | solution.py:421
  170.7 35.4 %collective-permute-start.24 = (bf16[1280,512]{1,0:T(8,128)(2,1)S(1)}, bf16[1280,512]{1,0:T(8,128)(2,1)}, u32[]{:S(2)}, u32[]{:S(2)}) collective-permute-start(bf16[1280,512]{1,0:T(8,128)(2,1)S(1)} %copy-done.3), channel_id=1, source_target_pairs={{0,64},{64,128},{128,192},{192,0},{1,65},{65,129},{129,193},{193,1... | collective-permute-start | bytes 3932168 | tf_op jit(solution)/shard_map/ppermute | solution.py:30
  173.3 1.2 collective-permute-start.23
  173.5 32.7 %collective-permute-start.16 = (bf16[512,1024]{1,0:T(8,128)(2,1)}, bf16[512,1024]{1,0:T(8,128)(2,1)}, u32[]{:S(2)}, u32[]{:S(2)}) collective-permute-start(bf16[512,1024]{1,0:T(8,128)(2,1)} %refs_2_), channel_id=1, source_target_pairs={{0,1},{1,0},{2,3},{3,2},{4,5},{5,4},{6,7},{7,6},{8,9},{9,8},{10,11... | collective-permute-start | bytes 3145736 | tf_op jit(solution)/shard_map/ppermute | solution.py:424
  174.5 31.6 %collective-permute-start.17 = (bf16[512,1024]{1,0:T(8,128)(2,1)}, bf16[512,1024]{1,0:T(8,128)(2,1)}, u32[]{:S(2)}, u32[]{:S(2)}) collective-permute-start(bf16[512,1024]{1,0:T(8,128)(2,1)} %collective-permute-done.refs_1_.refs_3_), channel_id=1, source_target_pairs={{0,1},{1,0},{2,3},{3,2},{4,5},{5,4},{6,7},{7,6},{8,9},{9,8},{10,11... | collective-permute-start | bytes 3145736 | tf_op jit(solution)/shard_map/ppermute | solution.py:424
  174.7 31.4 %collective-permute-start.18 = (bf16[512,1024]{1,0:T(8,128)(2,1)}, bf16[512,1024]{1,0:T(8,128)(2,1)}, u32[]{:S(2)}, u32[]{:S(2)}) collective-permute-start(bf16[512,1024]{1,0:T(8,128)(2,1)} %collective-permute-done.1.refs_2_.refs_4_), channel_id=1, source_target_pairs={{0,1},{1,0},{2,3},{3,2},{4,5},{5,4},{6,7},{7,6},{8,9},{9,8},{10,11... | collective-permute-start | bytes 3145736 | tf_op jit(solution)/shard_map/ppermute | solution.py:424
  175.0 31.1 %collective-permute-start.19 = (bf16[512,1024]{1,0:T(8,128)(2,1)}, bf16[512,1024]{1,0:T(8,128)(2,1)}, u32[]{:S(2)}, u32[]{:S(2)}) collective-permute-start(bf16[512,1024]{1,0:T(8,128)(2,1)} %collective-permute-done.2.refs_3_.refs_5_), channel_id=1, source_target_pairs={{0,1},{1,0},{2,3},{3,2},{4,5},{5,4},{6,7},{7,6},{8,9},{9,8},{10,11... | collective-permute-start | bytes 3145736 | tf_op jit(solution)/shard_map/ppermute | solution.py:424
  180.5 8.3 %copy-start.23 = (f32[128]{0:T(128)S(1)}, f32[128]{0:T(128)}, u32[]{:S(2)}) copy-start(f32[128]{0:T(128)} %param.37) | copy-start | bytes 1540
  180.5 8.3 %copy-start.24 = (f32[128]{0:T(128)S(1)}, f32[128]{0:T(128)}, u32[]{:S(2)}) copy-start(f32[128]{0:T(128)} %param.35) | copy-start | bytes 1540
  180.5 46.9 %all-to-all-start = ((bf16[32,16,640]{2,1,0:T(8,128)(2,1)}), bf16[32,16,640]{2,1,0:T(8,128)(2,1)S(1)}, u32[]{:S(2)}, u32[]{:S(2)}) async-start(bf16[32,16,640]{2,1,0:T(8,128)(2,1)} %shard_map.216), calls=%async_computation | async-start | bytes 1310720 | tf_op jit(solution)/shard_map/all_to_all | solution.py:499
  206.1 30.7 %collective-permute-start.27 = (bf16[1280,512]{1,0:T(8,128)(2,1)}, bf16[1280,512]{1,0:T(8,128)(2,1)S(1)}, u32[]{:S(2)}, u32[]{:S(2)}) collective-permute-start(bf16[1280,512]{1,0:T(8,128)(2,1)} %collective-permute-done.25.refs_16_), channel_id=1, source_target_pairs={{0,192},{64,0},{128,64},{192,128},{1,193},{65,1},{129,65},{193,129... | collective-permute-start | bytes 3932168 | tf_op jit(solution)/shard_map/ppermute | solution.py:30
  227.4 6.5 %copy-start = (bf16[32,16,640]{2,1,0:T(8,128)(2,1)}, bf16[32,16,640]{2,1,0:T(8,128)(2,1)S(1)}, u32[]{:S(2)}) copy-start(bf16[32,16,640]{2,1,0:T(8,128)(2,1)S(1)} %all-to-all-done.items_ref) | copy-start | bytes 1966084
  227.4 18.2 %all-to-all-start.1 = ((bf16[8,5,32,256]{3,2,1,0:T(8,128)(2,1)}), bf16[8,5,32,256]{3,2,1,0:T(8,128)(2,1)S(1)}, u32[]{:S(2)}, u32[]{:S(2)}) async-start(bf16[8,5,32,256]{3,2,1,0:T(8,128)(2,1)} %bitcast.125), calls=%async_computation.1 | async-start | bytes 1310720 | tf_op jit(solution)/shard_map/all_to_all | solution.py:511
  (10 other events, 28.0 us)
Sparse Core Ops, SparseCore 0:
  34.4 65.3 all-gather.1
where the time goes:
time: 260 us; the launch traced here: 257 us
  waiting for transfers between devices  84.8 us (33%)
  starting transfers between devices  68.4 us (26%)
  Pallas kernels  60.9 us (23%)
  local copies, waits for them, and re-layouts  15.8 us (6%)
  between operations  14.7 us (6%)
  other arithmetic  12.3 us (5%)
    ppermute x16, waiting for transfers between devices, shift(): lax.ppermute(a, axis, [(i, (i + by) % n) for i in range(n)])  50.7 us
    ppermute x6, starting transfers between devices, body(): lax.ppermute(a, 'tp', [(i, (i + 2 * by) % tp_ways) for i in range(tp_ways)])  35.1 us
    ppermute x6, waiting for transfers between devices, body(): lax.ppermute(a, 'tp', [(i, (i + 2 * by) % tp_ways) for i in range(tp_ways)])  31.6 us
    ppermute x16, starting transfers between devices, shift(): lax.ppermute(a, axis, [(i, (i + by) % n) for i in range(n)])  23.1 us
    pallas_call x1, Pallas kernels, vision_partial(): pl.pallas_call(vision_kernel, grid_spec=pltpu.PrefetchScalarGridSpec(num_...  16 us
    pallas_call x1, Pallas kernels, query_sums(): pl.pallas_call(lambda *refs: query_kernel(units, tail_units, *refs), grid...  10.9 us
    pallas_call x1, Pallas kernels, kv_rows(): pl.pallas_call(kv_kernel, grid_spec=pltpu.PrefetchScalarGridSpec(num_scal...  10.3 us
    pallas_call x3, Pallas kernels, place(): pl.pallas_call(place_kernel, grid_spec=pltpu.PrefetchScalarGridSpec(num_s...  9.18 us
  transfers between devices with their start and end apart: 31, of which 11 were waited for; matrix products, arithmetic and copies ran while one was open for 8% of the time, Pallas kernels for 21%

commit v1 on v0

v1 whole, which is shorter than its diff:
```python
import jax
import jax.numpy as jnp
from jax import lax
from jax.experimental import pallas as pl
from jax.experimental.pallas import tpu as pltpu
from jax.sharding import PartitionSpec as P

VD = 1280
VHD = 80
LANE = 128
HD = 128
EPS = 1e-06
CAP = 5
AHEAD = 3
WINDOW = 384
VMEM_LIMIT = 58 * 1024 * 1024


def resident():
    return pl.BlockSpec(memory_space=pltpu.VMEM)


def whole(shape):
    return pl.BlockSpec(shape, lambda *_: (0,) * len(shape))


def params(limit=VMEM_LIMIT):
    return pltpu.CompilerParams(vmem_limit_bytes=limit)


def cheap():
    return pl.CostEstimate(flops=1_000_000, bytes_accessed=1000, transcendentals=0)


def vision_kernel(own_ref, order_ref, patches_ref, gain_ref, w_ref, bias_ref, proj_ref, *refs):
    keep_ref, send_ref, resid_ref, w_pad, proj_pad, held, apart = refs[-7:]
    parts, span, width = held.shape
    total = parts * span
    chunks = w_ref.shape[0] // VHD
    core, chip = own_ref[0], own_ref[1]

    @pl.when(pl.program_id(0) == 0)
    def _():
        w_pad[...] = jnp.zeros_like(w_pad)
        proj_pad[...] = jnp.zeros_like(proj_pad)
        for pad, ref in ((w_pad, w_ref), (proj_pad, proj_ref)):
            for at in range(ref.shape[0] // VHD):
                pad[at * LANE : at * LANE + VHD] = ref[at * VHD : (at + 1) * VHD]
        window_q = (lax.broadcasted_iota(jnp.int32, (total, total), 0) & (span - 1)) >> 4
        window_k = (lax.broadcasted_iota(jnp.int32, (total, total), 1) & (span - 1)) >> 4
        apart[...] = jnp.where(window_q == window_k, 0.0, -1e30)

    places = patches_ref.shape[0]
    wanted = order_ref[...].reshape(total, 1)
    onehot = jnp.where(
        wanted == lax.broadcasted_iota(jnp.int32, (total, places), 1), 1.0, 0.0
    ).astype(jnp.bfloat16)
    rows = jnp.dot(onehot, patches_ref[...], preferred_element_type=jnp.float32)
    held[...] = rows.astype(jnp.bfloat16).reshape(parts, span, width)
    half = width // 2
    mine = pl.multiple_of(core * half, LANE)
    other = pl.multiple_of((1 - core) * half, LANE)
    resid_ref[...] = held[chip, :, pl.ds(mine, half)]
    factor = lax.rsqrt(jnp.mean(rows * rows, axis=-1, keepdims=True) + EPS)
    normed = (rows * factor * gain_ref[...][None, :]).astype(jnp.bfloat16)
    projected = lax.dot_general(
        normed, w_pad[...], (((1,), (1,)), ((), ())), preferred_element_type=jnp.float32
    )
    projected = (projected + bias_ref[...]).astype(jnp.bfloat16)
    heads = []
    for head in range(chunks // 3):
        at = head * 3 * LANE
        query = projected[:, at : at + LANE]
        keyed = projected[:, at + LANE : at + 2 * LANE]
        valued = projected[:, at + 2 * LANE : at + 3 * LANE]
        scores = lax.dot_general(
            query, keyed, (((1,), (1,)), ((), ())), preferred_element_type=jnp.float32
        )
        scores = scores * (VHD ** (-0.5)) + apart[...]
        raised = jnp.exp(scores - jnp.max(scores, axis=-1, keepdims=True))
        scale_back = 1.0 / jnp.sum(raised, axis=-1, keepdims=True)
        weights = raised.astype(jnp.bfloat16)
        mixed = jnp.dot(weights, valued, preferred_element_type=jnp.float32) * scale_back
        heads.append(mixed.astype(jnp.bfloat16))
    mixed = jnp.concatenate(heads, axis=1)
    for out_ref, at in ((keep_ref, mine), (send_ref, other)):
        part = jnp.dot(mixed, proj_pad[:, pl.ds(at, half)], preferred_element_type=jnp.float32)
        out_ref[...] = part.astype(jnp.bfloat16).reshape(parts, span, half)


def vision_partial(order, patches, gain, w, bias_pad, proj, own):
    parts, span, _ = order.shape
    width = patches.shape[1]
    step = 64
    half = width // 2
    chunks = w.shape[0] // VHD
    spec = pl.BlockSpec((parts, step, half), lambda i, _: (0, i, 0))
    out = jax.ShapeDtypeStruct((parts, span, half), jnp.bfloat16)
    return pl.pallas_call(
        vision_kernel,
        grid_spec=pltpu.PrefetchScalarGridSpec(
            num_scalar_prefetch=1,
            grid=(span // step,),
            in_specs=[
                pl.BlockSpec((parts, step, 1), lambda i, _: (0, i, 0)),
                whole(patches.shape),
                whole(gain.shape),
                whole(w.shape),
                whole(bias_pad.shape),
                whole(proj.shape),
            ],
            out_specs=[spec, spec, pl.BlockSpec((step, half), lambda i, _: (i, 0))],
            scratch_shapes=[
                pltpu.VMEM((chunks * LANE, width), jnp.bfloat16),
                pltpu.VMEM((chunks // 3 * LANE, width), jnp.bfloat16),
                pltpu.VMEM((parts, step, width), jnp.bfloat16),
                pltpu.VMEM((parts * step, parts * step), jnp.float32),
            ],
        ),
        out_shape=[out, out, jax.ShapeDtypeStruct((span, half), jnp.bfloat16)],
        compiler_params=params(),
        cost_estimate=pl.CostEstimate(
            flops=14_000_000_000, bytes_accessed=6_000_000, transcendentals=0
        ),
    )(own, order, patches, gain, w, bias_pad, proj)


def join_kernel(*refs):
    out_ref = refs[-1]
    at = 0
    for ref in refs[:-1]:
        out_ref[at : at + ref.shape[0]] = ref[...]
        at += ref.shape[0]


def join(*parts):
    shape = (sum(part.shape[0] for part in parts),) + parts[0].shape[1:]
    return pl.pallas_call(
        join_kernel,
        grid=(1,),
        in_specs=[whole(part.shape) for part in parts],
        out_specs=whole(shape),
        out_shape=jax.ShapeDtypeStruct(shape, parts[0].dtype),
        compiler_params=params(),
    )(*parts)


def scale_kernel(gain_ref, query_ref, key_ref, value_ref, out_ref):
    gain = gain_ref[...]
    at = 0
    for ref in (key_ref, value_ref, query_ref):
        width = ref.shape[1]
        scaled = ref[...].astype(jnp.float32) * gain
        out_ref[:, at : at + width] = scaled.astype(jnp.bfloat16)
        at += width


def scale(gain, w_query, w_key, w_value):
    parts = (gain, w_query, w_key, w_value)
    shape = (w_query.shape[0], sum(part.shape[1] for part in parts[1:]))
    return pl.pallas_call(
        scale_kernel,
        grid=(1,),
        in_specs=[whole(part.shape) for part in parts],
        out_specs=whole(shape),
        out_shape=jax.ShapeDtypeStruct(shape, jnp.bfloat16),
        compiler_params=params(),
    )(*parts)


def place_kernel(at_ref, items_ref, out_ref):
    out_ref[...] = jnp.zeros_like(out_ref)
    for index in range(items_ref.shape[0]):
        at = at_ref[index]

        @pl.when(at >= 0)
        def _():
            out_ref[pl.ds(at, 1)] = items_ref[index : index + 1]


def place(at, items, slots):
    shape = (slots,) + items.shape[1:]
    return pl.pallas_call(
        place_kernel,
        grid_spec=pltpu.PrefetchScalarGridSpec(
            num_scalar_prefetch=1,
            grid=(1,),
            in_specs=[whole(items.shape)],
            out_specs=whole(shape),
        ),
        out_shape=jax.ShapeDtypeStruct(shape, items.dtype),
        compiler_params=params(),
    )(at, items)


def rotary(values, cosine, sines):
    return values * cosine + pltpu.roll(values, HD // 2, 1) * sines


def anywhere():
    return pl.BlockSpec(memory_space=pl.ANY)


def order_kernel(ways_ref, *refs):
    x_refs, (out_ref, factor_ref, held, sems) = refs[:-4], refs[-4:]
    parts, rows, part = held.shape
    each = parts // len(x_refs)
    loads, stores = [], []
    for index in range(parts):
        at = index % each * rows
        source = x_refs[index // each].at[at : at + rows]
        loads.append(pltpu.make_async_copy(source, held.at[index], sems.at[index]))
        stores.append(
            pltpu.make_async_copy(
                held.at[index], out_ref.at[ways_ref[index]], sems.at[parts + index]
            )
        )
    for load in loads[:AHEAD]:
        load.start()
    squares = jnp.zeros((rows, LANE), jnp.float32)
    for index in range(parts):
        loads[index].wait()
        stores[index].start()
        for load in loads[index + AHEAD : index + AHEAD + 1]:
            load.start()
        for at in range(0, part, LANE):
            wide = held[index, :, at : at + LANE].astype(jnp.float32)
            squares += wide * wide
    squares = jnp.sum(squares, axis=-1, keepdims=True)
    factor_ref[...] = lax.rsqrt(squares / (parts * part) + EPS)
    for store in stores:
        store.wait()


def ordered(ways, rows, xs):
    parts, part = ways.shape[0], xs[0].shape[1]
    return pl.pallas_call(
        order_kernel,
        in_specs=[pl.BlockSpec(memory_space=pltpu.SMEM)] + [anywhere()] * len(xs),
        out_specs=[anywhere(), resident()],
        out_shape=[
            jax.ShapeDtypeStruct((parts, rows, part), jnp.bfloat16),
            jax.ShapeDtypeStruct((rows, 1), jnp.float32),
        ],
        scratch_shapes=[
            pltpu.VMEM((parts, rows, part), jnp.bfloat16),
            pltpu.SemaphoreType.DMA((2 * parts,)),
        ],
        compiler_params=params(),
        cost_estimate=cheap(),
    )(ways, *xs)


def kv_kernel(dest_ref, x_ref, w_ref, *refs):
    factor_ref, bias_ref, cos_ref, sin_ref, out_ref, pages_ref = refs[:6]
    x_held, held, sems = refs[6:]
    parts, rows, part = x_held.shape
    width = held.shape[2]
    loads = []
    for i in range(parts):
        rows_of = w_ref.at[i * part : (i + 1) * part, :width]
        loads.append(pltpu.make_async_copy(x_ref.at[i], x_held.at[i], sems.at[2 * i]))
        loads.append(pltpu.make_async_copy(rows_of, held.at[i], sems.at[2 * i + 1]))
    for copy in loads[: 2 * AHEAD]:
        copy.start()
    pages_ref[...] = jnp.zeros_like(pages_ref)
    total = jnp.zeros(out_ref.shape, jnp.float32)
    for index in range(parts):
        loads[2 * index].wait()
        loads[2 * index + 1].wait()
        for copy in loads[2 * (index + AHEAD) : 2 * (index + AHEAD + 1)]:
            copy.start()
        total += jnp.dot(x_held[index], held[index], preferred_element_type=jnp.float32)
    total = total * factor_ref[...] + bias_ref[...]
    out_ref[:, :HD] = rotary(total[:, :HD], cos_ref[...], sin_ref[...]).astype(jnp.bfloat16)
    out_ref[:, HD:] = total[:, HD:].astype(jnp.bfloat16)
    page_rows = pages_ref.shape[1]
    for page in range(rows // page_rows):
        pages_ref[pl.ds(dest_ref[page], 1)] = out_ref[
            page * page_rows : (page + 1) * page_rows, :
        ][None]


def kv_rows(dest, x, w, factor, bias, cosine, sines, slots, page_rows):
    parts, rows, part = x.shape
    width = bias.shape[1]
    small = (factor, bias, cosine, sines)
    shapes = [(rows, width), (slots, page_rows, width)]
    return pl.pallas_call(
        kv_kernel,
        in_specs=[pl.BlockSpec(memory_space=pltpu.SMEM)]
        + [anywhere()] * 2
        + [resident()] * len(small),
        out_specs=[resident()] * 2,
        out_shape=[jax.ShapeDtypeStruct(shape, jnp.bfloat16) for shape in shapes],
        scratch_shapes=[
            pltpu.VMEM(x.shape, jnp.bfloat16),
            pltpu.VMEM((parts, part, width), jnp.bfloat16),
            pltpu.SemaphoreType.DMA((2 * parts,)),
        ],
        compiler_params=params(),
        cost_estimate=pl.CostEstimate(
            flops=7_000_000_000, bytes_accessed=13_000_000, transcendentals=0
        ),
    )(dest, x, w, *small)


def attend_kernel(x_ref, w_ref, *refs):
    factor_ref, bias_ref, cos_ref, sin_ref, start_ref, kv_ref, out_ref = refs[:7]
    x_held, held, sems = refs[7:]
    parts, rows, part = x_held.shape
    skip = w_ref.shape[1] - held.shape[2]
    loads = []
    for i in range(parts):
        rows_of = w_ref.at[i * part : (i + 1) * part, skip:]
        loads.append(pltpu.make_async_copy(x_ref.at[i], x_held.at[i], sems.at[2 * i]))
        loads.append(pltpu.make_async_copy(rows_of, held.at[i], sems.at[2 * i + 1]))
    for copy in loads[: 2 * AHEAD]:
        copy.start()
    total = jnp.zeros(out_ref.shape, jnp.float32)
    for index in range(parts):
        loads[2 * index].wait()
        loads[2 * index + 1].wait()
        for copy in loads[2 * (index + AHEAD) : 2 * (index + AHEAD + 1)]:
            copy.start()
        total += jnp.dot(x_held[index], held[index], preferred_element_type=jnp.float32)
    total = total * factor_ref[...] + bias_ref[...]
    step = 256
    for first in range(0, rows, step):
        span = slice(first, first + step)
        begin = max(first + step - WINDOW, 0)
        end = first + step
        keyed = kv_ref[begin:end, :HD]
        valued = kv_ref[begin:end, HD:]
        key_at = begin + lax.broadcasted_iota(jnp.int32, (step, end - begin), 1)
        row_at = first + lax.broadcasted_iota(jnp.int32, (step, end - begin), 0)
        allowed = (key_at <= row_at) & (key_at >= start_ref[span, :])
        cosine, sines = cos_ref[span, :], sin_ref[span, :]
        for at in range(0, total.shape[1], HD):
            query = rotary(total[span, at : at + HD], cosine, sines).astype(jnp.bfloat16)
            scores = lax.dot_general(
                query, keyed, (((1,), (1,)), ((), ())), preferred_element_type=jnp.float32
            ) * (HD ** (-0.5))
            scores = jnp.where(allowed, scores, -1e30)
            raised = jnp.exp(scores - jnp.max(scores, axis=-1, keepdims=True))
            scale_back = 1.0 / jnp.sum(raised, axis=-1, keepdims=True)
            weights = raised.astype(jnp.bfloat16)
            mixed = jnp.dot(weights, valued, preferred_element_type=jnp.float32) * scale_back
            out_ref[span, at : at + HD] = mixed.astype(jnp.bfloat16)


def attend(x, w, factor, bias, cosine, sines, start, kv):
    parts, rows, part = x.shape
    width = bias.shape[1]
    small = (factor, bias, cosine, sines, start, kv)
    return pl.pallas_call(
        attend_kernel,
        in_specs=[anywhere()] * 2 + [resident()] * len(small),
        out_specs=resident(),
        out_shape=jax.ShapeDtypeStruct((rows, width), jnp.bfloat16),
        scratch_shapes=[
            pltpu.VMEM(x.shape, jnp.bfloat16),
            pltpu.VMEM((parts, part, width), jnp.bfloat16),
            pltpu.SemaphoreType.DMA((2 * parts,)),
        ],
        compiler_params=params(),
        cost_estimate=pl.CostEstimate(
            flops=14_000_000_000, bytes_accessed=17_000_000, transcendentals=0
        ),
    )(x, w, *small)


def after(values, *others):
    return lax.optimization_barrier((tuple(values),) + others)[0]


def body(
    patches, window_order, vis_gain, vis_qkv, vis_qkv_bias, vis_proj, vis_proj_bias, merge_gain,
    img_owner, img_slot, prompt_rows, lang_gain, w_query, b_query, w_key, b_key, w_value, b_value,
    page_owner, page_slot,
):
    phase, rep, tp = lax.axis_index("phase"), lax.axis_index("rep"), lax.axis_index("tp")
    n_phase, n_rep = lax.axis_size("phase"), lax.axis_size("rep")
    groups = n_phase * n_rep
    group = phase * n_rep + rep
    chip, core = tp // 2, tp % 2
    bf16, f32 = jnp.bfloat16, jnp.float32

    tp_ways = lax.axis_size("tp")
    chips = tp_ways // 2
    across = lambda a, by: lax.ppermute(
        a, "tp", [(i, (i + 2 * by) % tp_ways) for i in range(tp_ways)]
    )
    partner = lambda a: lax.ppermute(a, "tp", [(i, i ^ 1) for i in range(tp_ways)])
    take = lambda a, at: lax.dynamic_index_in_dim(a, at, 0, keepdims=False)

    owner, owners = img_owner[0], page_owner[0]

    depth = w_query.shape[0]
    gain = lax.dynamic_slice_in_dim(lang_gain, group * depth, depth)[:, None]
    own = scale(gain, w_query, w_key, w_value)

    weights = lax.all_gather(own, ("phase", "rep"), axis=0, tiled=True)
    x_near = [across(prompt_rows, by) for by in (1, -1)]

    patch_count, width = patches.shape
    merge = 4
    order = window_order[0].reshape(patch_count // merge, merge).T[:, :, None]
    chunks = vis_qkv.shape[1] // VHD
    bias_pad = jnp.pad(vis_qkv_bias.reshape(chunks, VHD), ((0, 0), (0, LANE - VHD))).reshape(1, -1)
    keep, send, resid = vision_partial(
        order, patches, vis_gain, vis_qkv.T, bias_pad, vis_proj, jnp.stack([core, chip])
    )
    keep, send, resid, x_own, *x_near = after((keep, send, resid, prompt_rows, *x_near))

    x_far = across(x_own, 2)
    chip_sum = (keep.astype(f32) + partner(send).astype(f32)).astype(bf16)
    dest_iota = jnp.arange(groups, dtype=jnp.int32)
    to_images = jnp.sum(
        jnp.where(owner[None, :] == dest_iota[:, None], img_slot + 1, 0), axis=1, keepdims=True
    )
    pages = owners.shape[0]
    rows = prompt_rows.shape[0]
    page_rows = rows // pages
    page_iota = jnp.arange(pages, dtype=jnp.int32)
    first_of = lambda ids: jnp.min(
        jnp.where(ids[..., :, None] == ids[..., None, :], page_iota, pages), axis=-1
    )
    first_page = first_of(owners)
    owner_group = phase * n_rep + owners
    hit = (owner_group[None, None, :] == dest_iota[:, None, None]) & (
        (page_iota - first_page)[None, None, :] == jnp.arange(7, dtype=jnp.int32)[None, :, None]
    )
    to_pages = jnp.sum(jnp.where(hit, page_slot[0] + 1, 0), axis=2)
    routes = lax.all_to_all(
        jnp.concatenate([to_images, to_pages], axis=1), ("phase", "rep"), split_axis=0,
        concat_axis=0, tiled=True,
    )
    start = jnp.repeat(first_page, page_rows) * page_rows
    position = jnp.arange(rows, dtype=jnp.int32) - start
    half_dim = HD // 2
    inv_freq = jnp.exp(-jnp.log(1000000.0) * jnp.arange(half_dim).astype(f32) / half_dim)
    angles = position.astype(f32)[:, None] * inv_freq[None, :]
    cosine, sines = jnp.cos(angles), jnp.sin(angles)
    cosine = jnp.concatenate([cosine, cosine], axis=1)
    sines = jnp.concatenate([-sines, sines], axis=1)
    chip_sum, x_far, x_own, routes, cosine, sines = after(
        (chip_sum, x_far, x_own, routes, cosine, sines)
    )

    arrived = [across(take(chip_sum, (chip + by) % chips), by) for by in (1, -1, 2)]
    x_side = join(x_own, *x_near, x_far)
    x_other = partner(x_side)
    half = width // 2
    cols = lambda a: lax.dynamic_slice_in_dim(a, core * half, half, a.ndim - 1)
    mixed = resid.astype(f32) + cols(vis_proj_bias)
    for part in [take(chip_sum, chip)] + arrived:
        mixed = mixed + part.astype(f32)
    squares = jnp.sum(mixed * mixed, axis=-1).reshape(2, -1)
    squares = squares + partner(squares)
    factor = lax.rsqrt(squares.reshape(-1, 1) / width + EPS)
    merged = (mixed * factor * cols(merge_gain)).astype(bf16)
    requests = owner.shape[0]
    merged = merged.reshape(requests, -1, half)
    outgoing = place(owner, merged, groups)
    outgoing, x_other = after((outgoing, x_other))

    images = lax.all_to_all(outgoing, ("phase", "rep"), split_axis=0, concat_axis=0, tiled=True)
    ways = jnp.stack(
        [((chip - by) % chips) * 2 + side for side in (core, 1 - core) for by in (0, 1, -1, 2)]
    ).astype(jnp.int32)
    x, row_factor = ordered(ways, rows, (x_side, x_other))

    image_at = routes[:, 0] - 1
    page_at = lax.dynamic_slice_in_dim(routes, phase * n_rep, n_rep, 0)[:, 1 : 1 + CAP] - 1
    page_at = page_at.reshape(-1)
    image_buffer = place(image_at, images, groups).reshape(-1, half)
    dest = (owners * CAP + page_iota - first_page).astype(jnp.int32)
    weights, image_buffer, page_at, start, x, row_factor, dest = after(
        (weights, image_buffer, page_at, start[:, None], x, row_factor, dest)
    )

    kv, outgoing_pages = kv_rows(
        dest, x, weights, row_factor, jnp.concatenate([b_key, b_value])[None, :], cosine, sines,
        n_rep * CAP, page_rows,
    )
    arrived_pages = lax.all_to_all(
        outgoing_pages.reshape(n_rep, CAP, page_rows, -1), "rep", split_axis=0, concat_axis=0, tiled=True
    )
    attn_out = attend(x, weights, row_factor, b_query[None, :], cosine, sines, start, kv)
    kv_pool = place(page_at, arrived_pages.reshape(n_rep * CAP, page_rows, -1), pages)
    return (image_buffer, attn_out, kv_pool)


def solution(mesh):
    split, cut = P(("phase", "rep"), None), P(("phase", "rep"), "tp")
    return jax.shard_map(
        body,
        mesh=mesh,
        in_specs=(
            split, split, P(), P(None, "tp"), P("tp"), P("tp", None), P(), P(), split, split,
            cut, P(), cut, P("tp"), cut, P("tp"), cut, P("tp"), split, split,
        ),
        out_specs=(cut, cut, P(("phase", "rep"), None, "tp")),
        check_vma=False,
    )
```

time: 260 us -> 192 us (0.74)
  starting transfers between devices: 68.4 us -> 36.5 us
  waiting for transfers between devices: 84.8 us -> 61.4 us
  local copies, waits for them, and re-layouts: 15.8 us -> 11.3 us
  other arithmetic: 12.3 us -> 8.73 us
    ppermute x16 -> x0, waiting for transfers between devices: 50.7 us -> none  [shift(): lax.ppermute(a, axis, [(i, (i + by) % n) for i in range(n)])]
    ppermute x6, starting transfers between devices: 35.1 us -> 9.03 us  [body(): lax.ppermute(a, 'tp', [(i, (i + 2 * by) % tp_ways) for i in range(tp_ways)])]
    ppermute x16 -> x0, starting transfers between devices: 23.1 us -> none  [shift(): lax.ppermute(a, axis, [(i, (i + by) % n) for i in range(n)])]
    all_to_all x1, waiting for transfers between devices: 0.01 us -> 15.2 us  [body(): lax.all_to_all(outgoing, ('phase', 'rep'), split_axis=0, concat_axis=0, t...]
    all_to_all x0 -> x1, starting transfers between devices: none -> 11.6 us  [body(): lax.all_to_all(jnp.concatenate([to_images, to_pages], axis=1), ('phase',...]
    all_gather x1, waiting for transfers between devices: 0.02 us -> 10.6 us  [body(): weights = lax.all_gather(own, ('phase', 'rep'), axis=0, tiled=True)]
    ppermute x6, waiting for transfers between devices: 31.6 us -> 21.4 us  [body(): lax.ppermute(a, 'tp', [(i, (i + 2 * by) % tp_ways) for i in range(tp_ways)])]
    all_to_all x1, starting transfers between devices: 5.15 us -> 11.2 us  [body(): lax.all_to_all(outgoing, ('phase', 'rep'), split_axis=0, concat_axis=0, t...]
  transfers between devices with their start and end apart: 31 -> 13, of which waited for: 11 -> 11; matrix products, arithmetic and copies ran while one was open for 8% -> 9% of each run, Pallas kernels for 21% -> 24%
where the time goes in v1:
time: 192 us; the launch traced here: 191 us
  waiting for transfers between devices  61.4 us (32%)
  Pallas kernels  58.9 us (31%)
  starting transfers between devices  36.5 us (19%)
  between operations  14.4 us (8%)
  local copies, waits for them, and re-layouts  11.3 us (6%)
  other arithmetic  8.73 us (5%)
    ppermute x6, waiting for transfers between devices, body(): lax.ppermute(a, 'tp', [(i, (i + 2 * by) % tp_ways) for i in range(tp_ways)])  21.4 us
    all_to_all x1, waiting for transfers between devices, body(): lax.all_to_all(outgoing, ('phase', 'rep'), split_axis=0, concat_axis=0, t...  15.2 us
    pallas_call x1, Pallas kernels, vision_partial(): pl.pallas_call(vision_kernel, grid_spec=pltpu.PrefetchScalarGridSpec(num_...  14.4 us
    all_to_all x1, starting transfers between devices, body(): lax.all_to_all(jnp.concatenate([to_images, to_pages], axis=1), ('phase',...  11.6 us
    pallas_call x1, Pallas kernels, attend(): pl.pallas_call(attend_kernel, in_specs=[anywhere()] * 2 + [resident()] *...  11.6 us
    all_to_all x1, starting transfers between devices, body(): lax.all_to_all(outgoing, ('phase', 'rep'), split_axis=0, concat_axis=0, t...  11.2 us
    all_gather x1, waiting for transfers between devices, body(): weights = lax.all_gather(own, ('phase', 'rep'), axis=0, tiled=True)  10.6 us
    ppermute x6, starting transfers between devices, body(): lax.ppermute(a, 'tp', [(i, (i + 2 * by) % tp_ways) for i in range(tp_ways)])  9.03 us
  transfers between devices with their start and end apart: 13, of which 11 were waited for; matrix products, arithmetic and copies ran while one was open for 9% of the time, Pallas kernels for 24%

profile of v1, /device:TPU:2, one launch (start us, length us, event | category | flops | bytes accessed | tf_op | source)
XLA Modules:
  0.0 191.2 jit_solution(4677254362081701041)
XLA Ops:
  7.3 0.8 dynamic_slice.25
  8.0 0.8 copy.34.gain_ref
  8.8 1.9 %shard_map.211 = bf16[256,768]{1,0:T(8,128)(2,1)} custom-call(f32[256,1]{1,0:T(8,128)} %copy.34.gain_ref, bf16[256,512]{1,0:T(8,128)(2,1)} %query_ref.1, bf16[256,128]{1,0:T(8,128)(2,1)} %key_ref.1, bf16[256,128]{1,0:T(8,128)(2,1)} %value_ref.1), custom_call_target="tpu_custom_call" | custom-call | tf_op jit(solution)/shard_map/pallas_call | solution.py:161
  10.8 1.6 collective-permute-start
  12.3 0.9 collective-permute-start.1
  13.7 0.7 reduce.5
  14.5 2.7 %copy.36.order_ref = s32[4,256,1]{2,1,0:T(8,128)} copy(s32[4,256,1]{0,1,2:T(8,128)S(1)} %bitcast.59) | data formatting | bytes 8192 | tf_op jit(solution)/shard_map/broadcast_in_dim | solution.py:408
  17.3 0.6 copy.43
  17.9 0.6 pad_add_fusion.1.own_ref
  18.7 0.6 add_subtract_fusion
  19.4 14.4 %shard_map.212 = (bf16[4,256,640]{2,1,0:T(8,128)(2,1)}, bf16[4,256,640]{2,1,0:T(8,128)(2,1)}, bf16[256,640]{1,0:T(8,128)(2,1)}) custom-call(s32[2]{0:T(128)} %pad_add_fusion.1.own_ref, s32[4,256,1]{2,1,0:T(8,128)} %copy.36.order_ref, bf16[1024,1280]{1,0:T(8,128)(2,1)} %patches_ref.1, f32[1280]{0:T(1024)} %gain_ref.1, bf16[480,1280]{1,0:T(8,128)(2,1)} %bitcast.70, ...), custom_call_target="tpu_custom_call" | custom-call | flops 14000000000 | bytes 6000000 | tf_op jit(solution)/shard_map/pallas_call | solution.py:99
  33.7 2.2 %collective-permute-done.refs_1_ = bf16[512,1024]{1,0:T(8,128)(2,1)S(1)} collective-permute-done((bf16[512,1024]{1,0:T(8,128)(2,1)}, bf16[512,1024]{1,0:T(8,128)(2,1)S(1)}, u32[]{:S(2)}, u32[]{:S(2)}) %collective-permute-start) | collective-permute-done | bytes 1048608 | tf_op jit(solution)/shard_map/ppermute | solution.py:391
  36.0 1.3 collective-permute-done.1.refs_2_
  37.6 2.3 %collective-permute-start.3 = (bf16[512,1024]{1,0:T(8,128)(2,1)}, bf16[512,1024]{1,0:T(8,128)(2,1)}, u32[]{:S(2)}, u32[]{:S(2)}) collective-permute-start(bf16[512,1024]{1,0:T(8,128)(2,1)} %refs_0_), channel_id=1, source_target_pairs={{0,4},{1,5},{2,6},{3,7},{4,0},{5,1},{6,2},{7,3},{8,12},{9,13},{10,... | collective-permute-start | bytes 3145736 | tf_op jit(solution)/shard_map/ppermute | solution.py:391
  39.9 0.7 copy.37
  40.6 11.6 %all-to-all-start = ((s32[32,1,8]{2,1,0:T(1,128)}), s32[32,1,8]{2,1,0:T(1,128)S(1)}, u32[]{:S(2)}, u32[]{:S(2)}) async-start(s32[32,1,8]{2,1,0:T(1,128)} %bitcast.11), calls=%async_computation | async-start | bytes 32768 | tf_op jit(solution)/shard_map/all_to_all | solution.py:435
  52.3 1.0 fusion.3
  53.3 1.0 pad_maximum_fusion
  54.4 1.6 add_convert_fusion
  56.0 5.9 %all-to-all-done = s32[32,1,8]{2,1,0:T(1,128)S(1)} async-done(((s32[32,1,8]{2,1,0:T(1,128)}), s32[32,1,8]{2,1,0:T(1,128)S(1)}, u32[]{:S(2)}, u32[]{:S(2)}) %all-to-all-start) | async-done | bytes 1056 | tf_op jit(solution)/shard_map/all_to_all | solution.py:435
  61.9 3.2 %collective-permute-done.3.refs_3_ = bf16[512,1024]{1,0:T(8,128)(2,1)} collective-permute-done((bf16[512,1024]{1,0:T(8,128)(2,1)}, bf16[512,1024]{1,0:T(8,128)(2,1)}, u32[]{:S(2)}, u32[]{:S(2)}) %collective-permute-start.3) | collective-permute-done | bytes 1048608 | tf_op jit(solution)/shard_map/ppermute | solution.py:391
  65.0 5.0 %shard_map.214.refs_0_ = bf16[2048,1024]{1,0:T(8,128)(2,1)} custom-call(bf16[512,1024]{1,0:T(8,128)(2,1)} %refs_0_, bf16[512,1024]{1,0:T(8,128)(2,1)} %copy-done.4, bf16[512,1024]{1,0:T(8,128)(2,1)} %collective-permute-done.1.refs_2_, bf16[512,1024]{1,0:T(8,128)(2,1)} %collective-permute-done.3.refs_3_), custom_call_target="tpu_custom_call" | custom-call | tf_op jit(solution)/shard_map/pallas_call | solution.py:138
  70.1 0.8 dynamic-slice_bitcast_fusion.2
  71.0 1.1 collective-permute-start.4
  72.0 1.0 collective-permute-start.5
  73.0 2.3 %collective-permute-start.6 = (bf16[256,640]{1,0:T(8,128)(2,1)S(1)}, bf16[256,640]{1,0:T(8,128)(2,1)S(1)}, u32[]{:S(2)}, u32[]{:S(2)}) collective-permute-start(bf16[256,640]{1,0:T(8,128)(2,1)S(1)} %get-tuple-element.60), channel_id=1, source_target_pairs={{0,4},{1,5},{2,6},{3,7},{4,0},{5,1},{6,2},{7,3},{8,12},{9,13},{10,... | collective-permute-start | bytes 983048 | tf_op jit(solution)/shard_map/ppermute | solution.py:391
  75.3 6.4 %collective-permute-done.4 = bf16[256,640]{1,0:T(8,128)(2,1)S(1)} collective-permute-done((bf16[256,640]{1,0:T(8,128)(2,1)}, bf16[256,640]{1,0:T(8,128)(2,1)S(1)}, u32[]{:S(2)}, u32[]{:S(2)}) %collective-permute-start.4) | collective-permute-done | bytes 327712 | tf_op jit(solution)/shard_map/ppermute | solution.py:391
  81.8 8.2 %collective-permute-done.6 = bf16[256,640]{1,0:T(8,128)(2,1)S(1)} collective-permute-done((bf16[256,640]{1,0:T(8,128)(2,1)S(1)}, bf16[256,640]{1,0:T(8,128)(2,1)S(1)}, u32[]{:S(2)}, u32[]{:S(2)}) %collective-permute-start.6) | collective-permute-done | bytes 327712 | tf_op jit(solution)/shard_map/ppermute | solution.py:391
  90.7 1.0 collective-permute-done.7
  91.8 1.0 multiply_convert_fusion
  92.8 2.8 %shard_map.213 = bf16[32,16,640]{2,1,0:T(8,128)(2,1)} custom-call(s32[16]{0:T(128)} %bitcast.66, bf16[16,16,640]{2,1,0:T(8,128)(2,1)} %bitcast.56), custom_call_target="tpu_custom_call" | custom-call | tf_op jit(solution)/shard_map/pallas_call | solution.py:183
  95.6 11.2 %all-to-all-start.1 = ((bf16[32,16,640]{2,1,0:T(8,128)(2,1)}), bf16[32,16,640]{2,1,0:T(8,128)(2,1)S(1)}, u32[]{:S(2)}, u32[]{:S(2)}) async-start(bf16[32,16,640]{2,1,0:T(8,128)(2,1)} %shard_map.213), calls=%async_computation.1 | async-start | bytes 1310720 | tf_op jit(solution)/shard_map/all_to_all | solution.py:468
  106.9 0.6 stack.47.ways_ref
  107.5 0.6 pad_maximum_fusion.2
  108.1 0.6 reshape.149.at_ref
  108.7 0.7 add_reduce_fusion.at_ref
  109.4 8.6 %shard_map.216 = (bf16[8,512,1024]{2,1,0:T(8,128)(2,1)}, f32[512,1]{1,0:T(8,128)}) custom-call(s32[8]{0:T(128)} %stack.47.ways_ref, bf16[2048,1024]{1,0:T(8,128)(2,1)} %shard_map.214.refs_0_, bf16[2048,1024]{1,0:T(8,128)(2,1)} %collective-permute-done.8.refs_1_), custom_call_target="tpu_custom_call" | custom-call | flops 1000000 | bytes 1000 | tf_op jit(solution)/shard_map/pallas_call | solution.py:237
  118.0 15.2 %all-to-all-done.1.items_ref = bf16[32,16,640]{2,1,0:T(8,128)(2,1)S(1)} async-done(((bf16[32,16,640]{2,1,0:T(8,128)(2,1)}), bf16[32,16,640]{2,1,0:T(8,128)(2,1)S(1)}, u32[]{:S(2)}, u32[]{:S(2)}) %all-to-all-start.1) | async-done | bytes 655392 | tf_op jit(solution)/shard_map/all_to_all | solution.py:468
  133.3 0.9 copy-done
  134.1 2.9 %shard_map.215 = bf16[32,16,640]{2,1,0:T(8,128)(2,1)} custom-call(s32[32]{0:T(128)} %add_reduce_fusion.at_ref, bf16[32,16,640]{2,1,0:T(8,128)(2,1)} %copy-done), custom_call_target="tpu_custom_call" | custom-call | tf_op jit(solution)/shard_map/pallas_call | solution.py:183
  137.0 10.6 %all-gather.2.cloned.1.call-done.w_ref = bf16[8192,768]{1,0:T(8,128)(2,1)} async-done(((bf16[256,768]{1,0:T(8,128)(2,1)}), bf16[8192,768]{1,0:T(8,128)(2,1)}) %all-gather.2.cloned.1.call-update) | async-done | bytes 12582928 | tf_op jit(solution)/shard_map/all_gather | solution.py:403
  147.6 9.0 %shard_map.217 = (bf16[512,256]{1,0:T(8,128)(2,1)}, bf16[40,32,256]{2,1,0:T(8,128)(2,1)}) custom-call(s32[16]{0:T(128)} %get-tuple-element.55.dest_ref, bf16[8,512,1024]{2,1,0:T(8,128)(2,1)} %get-tuple-element.49.x_ref, bf16[8192,768]{1,0:T(8,128)(2,1)} %all-gather.2.cloned.1.call-done.w_ref, f32[512,1]{1,0:T(8,128)} %get-tuple-element.51.refs_0_, ...), custom_call_target="tpu_custom_call" | custom-call | flops 7000000000 | bytes 13000000 | tf_op jit(solution)/shard_map/pallas_call | solution.py:289
  156.6 4.4 %all-to-all-start.2 = ((bf16[8,5,32,256]{3,2,1,0:T(8,128)(2,1)}), bf16[8,5,32,256]{3,2,1,0:T(8,128)(2,1)S(1)}, u32[]{:S(2)}, u32[]{:S(2)}) async-start(bf16[8,5,32,256]{3,2,1,0:T(8,128)(2,1)} %bitcast.58), calls=%async_computation.2 | async-start | bytes 1310720 | tf_op jit(solution)/shard_map/all_to_all | solution.py:487
  161.0 0.9 copy.38.refs_4_
  161.9 11.6 %shard_map.218 = bf16[512,512]{1,0:T(8,128)(2,1)} custom-call(bf16[8,512,1024]{2,1,0:T(8,128)(2,1)} %get-tuple-element.49.x_ref, bf16[8192,768]{1,0:T(8,128)(2,1)} %all-gather.2.cloned.1.call-done.w_ref, f32[512,1]{1,0:T(8,128)} %get-tuple-element.51.refs_0_, f32[1,512]{1,0:T(1,128)} %bitcast.71, f32[512,128]{1,0:T(8,128)} %get-tuple-element.52.refs_2_, ...), custom_call_target="tpu_custom_call" | custom-call | flops 14000000000 | bytes 17000000 | tf_op jit(solution)/shard_map/pallas_call | solution.py:356
  173.5 7.2 %all-to-all-done.2 = bf16[8,5,32,256]{3,2,1,0:T(8,128)(2,1)S(1)} async-done(((bf16[8,5,32,256]{3,2,1,0:T(8,128)(2,1)}), bf16[8,5,32,256]{3,2,1,0:T(8,128)(2,1)S(1)}, u32[]{:S(2)}, u32[]{:S(2)}) %all-to-all-start.2) | async-done | bytes 655392 | tf_op jit(solution)/shard_map/all_to_all | solution.py:487
  180.7 0.9 copy-done.1
  181.5 2.8 %shard_map.219 = bf16[16,32,256]{2,1,0:T(8,128)(2,1)} custom-call(s32[40]{0:T(128)} %reshape.149.at_ref, bf16[40,32,256]{2,1,0:T(8,128)(2,1)} %bitcast.55), custom_call_target="tpu_custom_call" | custom-call | tf_op jit(solution)/shard_map/pallas_call | solution.py:183
  (59 shorter events, 2.5 us)
Async XLA Ops:
  7.2 6.6 %copy-start.5 = (s32[1,1024]{1,0:T(1,128)S(1)}, s32[1,1024]{1,0:T(1,128)}, u32[]{:S(2)}) copy-start(s32[1,1024]{1,0:T(1,128)} %param.21) | copy-start | bytes 12292
  7.2 10.0 %copy-start.6 = (f32[480]{0:T(512)S(1)}, f32[480]{0:T(512)}, u32[]{:S(2)}) copy-start(f32[480]{0:T(512)} %param.24) | copy-start | bytes 5764
  7.2 11.4 %copy-start.10 = (s32[1,16]{1,0:T(1,128)S(1)}, s32[1,16]{1,0:T(1,128)}, u32[]{:S(2)}) copy-start(s32[1,16]{1,0:T(1,128)} %param.38) | copy-start | bytes 196
  7.2 11.5 %copy-start.13 = (s32[1,16]{1,0:T(1,128)S(1)}, s32[1,16]{1,0:T(1,128)}, u32[]{:S(2)}) copy-start(s32[1,16]{1,0:T(1,128)} %param.39) | copy-start | bytes 196
  7.2 140.4 %all-gather.2.cloned.1.call-start = ((), (), s32[]{:S(2)}) async-start(), calls=%async_computation.3 | async-start | bytes 12976128 | tf_op jit(solution)/shard_map/all_gather | solution.py:403
  10.8 25.2 %collective-permute-start = (bf16[512,1024]{1,0:T(8,128)(2,1)}, bf16[512,1024]{1,0:T(8,128)(2,1)S(1)}, u32[]{:S(2)}, u32[]{:S(2)}) collective-permute-start(bf16[512,1024]{1,0:T(8,128)(2,1)} %refs_0_), channel_id=1, source_target_pairs={{0,2},{1,3},{2,4},{3,5},{4,6},{5,7},{6,0},{7,1},{8,10},{9,11},{10,... | collective-permute-start | bytes 3145736 | tf_op jit(solution)/shard_map/ppermute | solution.py:391
  12.3 24.9 %collective-permute-start.1 = (bf16[512,1024]{1,0:T(8,128)(2,1)}, bf16[512,1024]{1,0:T(8,128)(2,1)}, u32[]{:S(2)}, u32[]{:S(2)}) collective-permute-start(bf16[512,1024]{1,0:T(8,128)(2,1)} %refs_0_), channel_id=1, source_target_pairs={{0,6},{1,7},{2,0},{3,1},{4,2},{5,3},{6,4},{7,5},{8,14},{9,15},{10,... | collective-permute-start | bytes 3145736 | tf_op jit(solution)/shard_map/ppermute | solution.py:391
  19.3 17.9 %copy-start.14 = (s32[1,16]{1,0:T(1,128)S(1)}, s32[1,16]{1,0:T(1,128)}, u32[]{:S(2)}) copy-start(s32[1,16]{1,0:T(1,128)} %param.29) | copy-start | bytes 196
  19.4 17.9 %copy-start.9 = (s32[1,16]{1,0:T(1,128)S(1)}, s32[1,16]{1,0:T(1,128)}, u32[]{:S(2)}) copy-start(s32[1,16]{1,0:T(1,128)} %param.28) | copy-start | bytes 196
  33.7 20.7 %copy-start.2 = (bf16[4,256,640]{2,1,0:T(8,128)(2,1)S(1)}, bf16[4,256,640]{2,1,0:T(8,128)(2,1)}, u32[]{:S(2)}) copy-start(bf16[4,256,640]{2,1,0:T(8,128)(2,1)} %get-tuple-element.34) | copy-start | bytes 3932164
  36.0 18.4 %copy-start.4 = (bf16[512,1024]{1,0:T(8,128)(2,1)}, bf16[512,1024]{1,0:T(8,128)(2,1)S(1)}, u32[]{:S(2)}) copy-start(bf16[512,1024]{1,0:T(8,128)(2,1)S(1)} %collective-permute-done.refs_1_) | copy-start | bytes 3145732
  37.3 17.1 %collective-permute-start.2 = (bf16[4,256,640]{2,1,0:T(8,128)(2,1)}, bf16[4,256,640]{2,1,0:T(8,128)(2,1)}, u32[]{:S(2)}, u32[]{:S(2)}) collective-permute-start(bf16[4,256,640]{2,1,0:T(8,128)(2,1)} %get-tuple-element.35), channel_id=1, source_target_pairs={{0,1},{1,0},{2,3},{3,2},{4,5},{5,4},{6,7},{7,6},{8,9},{9,8},{10,11... | collective-permute-start | bytes 3932168 | tf_op jit(solution)/shard_map/ppermute | solution.py:394
  37.6 27.5 %collective-permute-start.3 = (bf16[512,1024]{1,0:T(8,128)(2,1)}, bf16[512,1024]{1,0:T(8,128)(2,1)}, u32[]{:S(2)}, u32[]{:S(2)}) collective-permute-start(bf16[512,1024]{1,0:T(8,128)(2,1)} %refs_0_), channel_id=1, source_target_pairs={{0,4},{1,5},{2,6},{3,7},{4,0},{5,1},{6,2},{7,3},{8,12},{9,13},{10,... | collective-permute-start | bytes 3145736 | tf_op jit(solution)/shard_map/ppermute | solution.py:391
  40.6 21.3 %all-to-all-start = ((s32[32,1,8]{2,1,0:T(1,128)}), s32[32,1,8]{2,1,0:T(1,128)S(1)}, u32[]{:S(2)}, u32[]{:S(2)}) async-start(s32[32,1,8]{2,1,0:T(1,128)} %bitcast.11), calls=%async_computation | async-start | bytes 32768 | tf_op jit(solution)/shard_map/all_to_all | solution.py:435
  70.1 5.2 %copy-start.7 = (f32[1280]{0:T(1024)S(1)}, f32[1280]{0:T(1024)}, u32[]{:S(2)}) copy-start(f32[1280]{0:T(1024)} %param.26) | copy-start | bytes 15364
  70.1 20.0 %copy-start.3 = (bf16[256,640]{1,0:T(8,128)(2,1)S(1)}, bf16[256,640]{1,0:T(8,128)(2,1)}, u32[]{:S(2)}) copy-start(bf16[256,640]{1,0:T(8,128)(2,1)} %get-tuple-element.38) | copy-start | bytes 983044
  70.1 25.5 %collective-permute-start.8 = (bf16[2048,1024]{1,0:T(8,128)(2,1)}, bf16[2048,1024]{1,0:T(8,128)(2,1)}, u32[]{:S(2)}, u32[]{:S(2)}) collective-permute-start(bf16[2048,1024]{1,0:T(8,128)(2,1)} %shard_map.214.refs_0_), channel_id=1, source_target_pairs={{0,1},{1,0},{2,3},{3,2},{4,5},{5,4},{6,7},{7,6},{8,9},{9,8},{10,11... | collective-permute-start | bytes 12582920 | tf_op jit(solution)/shard_map/ppermute | solution.py:394
  71.0 19.7 %copy-start.8 = (f32[1280]{0:T(1024)S(1)}, f32[1280]{0:T(1024)}, u32[]{:S(2)}) copy-start(f32[1280]{0:T(1024)} %param.27) | copy-start | bytes 15364
  71.0 10.7 %collective-permute-start.4 = (bf16[256,640]{1,0:T(8,128)(2,1)}, bf16[256,640]{1,0:T(8,128)(2,1)S(1)}, u32[]{:S(2)}, u32[]{:S(2)}) collective-permute-start(bf16[256,640]{1,0:T(8,128)(2,1)} %get-tuple-element.59), channel_id=1, source_target_pairs={{0,2},{1,3},{2,4},{3,5},{4,6},{5,7},{6,0},{7,1},{8,10},{9,11},{10,... | collective-permute-start | bytes 983048 | tf_op jit(solution)/shard_map/ppermute | solution.py:391
  72.0 9.8 %collective-permute-start.5 = (bf16[256,640]{1,0:T(8,128)(2,1)S(1)}, bf16[256,640]{1,0:T(8,128)(2,1)S(1)}, u32[]{:S(2)}, u32[]{:S(2)}) collective-permute-start(bf16[256,640]{1,0:T(8,128)(2,1)S(1)} %get-tuple-element.61), channel_id=1, source_target_pairs={{0,6},{1,7},{2,0},{3,1},{4,2},{5,3},{6,4},{7,5},{8,14},{9,15},{10,... | collective-permute-start | bytes 983048 | tf_op jit(solution)/shard_map/ppermute | solution.py:391
  73.0 17.0 %collective-permute-start.6 = (bf16[256,640]{1,0:T(8,128)(2,1)S(1)}, bf16[256,640]{1,0:T(8,128)(2,1)S(1)}, u32[]{:S(2)}, u32[]{:S(2)}) collective-permute-start(bf16[256,640]{1,0:T(8,128)(2,1)S(1)} %get-tuple-element.60), channel_id=1, source_target_pairs={{0,4},{1,5},{2,6},{3,7},{4,0},{5,1},{6,2},{7,3},{8,12},{9,13},{10,... | collective-permute-start | bytes 983048 | tf_op jit(solution)/shard_map/ppermute | solution.py:391
  90.4 1.4 collective-permute-start.7
  92.8 14.7 %copy-start.11 = (f32[128]{0:T(128)S(1)}, f32[128]{0:T(128)}, u32[]{:S(2)}) copy-start(f32[128]{0:T(128)} %param.37) | copy-start | bytes 1540
  92.8 14.7 %copy-start.12 = (f32[128]{0:T(128)S(1)}, f32[128]{0:T(128)}, u32[]{:S(2)}) copy-start(f32[128]{0:T(128)} %param.35) | copy-start | bytes 1540
  95.6 37.7 %all-to-all-start.1 = ((bf16[32,16,640]{2,1,0:T(8,128)(2,1)}), bf16[32,16,640]{2,1,0:T(8,128)(2,1)S(1)}, u32[]{:S(2)}, u32[]{:S(2)}) async-start(bf16[32,16,640]{2,1,0:T(8,128)(2,1)} %shard_map.213), calls=%async_computation.1 | async-start | bytes 1310720 | tf_op jit(solution)/shard_map/all_to_all | solution.py:468
  133.3 0.9 copy-start
  156.6 24.1 %all-to-all-start.2 = ((bf16[8,5,32,256]{3,2,1,0:T(8,128)(2,1)}), bf16[8,5,32,256]{3,2,1,0:T(8,128)(2,1)S(1)}, u32[]{:S(2)}, u32[]{:S(2)}) async-start(bf16[8,5,32,256]{3,2,1,0:T(8,128)(2,1)} %bitcast.58), calls=%async_computation.2 | async-start | bytes 1310720 | tf_op jit(solution)/shard_map/all_to_all | solution.py:487
  180.7 0.9 copy-start.1
Sparse Core Ops, SparseCore 0:
  10.9 136.6 all-gather.1

commit v2 on v1

--- a/solution.py
+++ b/solution.py
@@ -189,6 +189,36 @@
             out_specs=whole(shape),
         ),
         out_shape=jax.ShapeDtypeStruct(shape, items.dtype),
+        compiler_params=params(),
+    )(at, items)
+
+
+def pool_kernel(at_ref, items_ref, out_ref, sems):
+    def copy(index):
+        return pltpu.make_async_copy(
+            items_ref.at[index], out_ref.at[at_ref[index]], sems.at[index]
+        )
+
+    for index in range(items_ref.shape[0]):
+
+        @pl.when(at_ref[index] >= 0)
+        def _():
+            copy(index).start()
+
+    for index in range(items_ref.shape[0]):
+
+        @pl.when(at_ref[index] >= 0)
+        def _():
+            copy(index).wait()
+
+
+def pool(at, items, slots):
+    return pl.pallas_call(
+        pool_kernel,
+        in_specs=[pl.BlockSpec(memory_space=pltpu.SMEM), anywhere()],
+        out_specs=anywhere(),
+        out_shape=jax.ShapeDtypeStruct((slots,) + items.shape[1:], items.dtype),
+        scratch_shapes=[pltpu.SemaphoreType.DMA((items.shape[0],))],
         compiler_params=params(),
     )(at, items)
 
@@ -448,9 +478,14 @@
         (chip_sum, x_far, x_own, routes, cosine, sines)
     )
 
+    x_side = join(x_own, *x_near, x_far)
+    ways = jnp.stack(
+        [((chip - by) % chips) * 2 + side for side in (core, 1 - core) for by in (0, 1, -1, 2)]
+    ).astype(jnp.int32)
+    x, row_factor = ordered(ways, rows, (x_side, partner(x_side)))
+    chip_sum, x, row_factor = after((chip_sum, x, row_factor))
+
     arrived = [across(take(chip_sum, (chip + by) % chips), by) for by in (1, -1, 2)]
-    x_side = join(x_own, *x_near, x_far)
-    x_other = partner(x_side)
     half = width // 2
     cols = lambda a: lax.dynamic_slice_in_dim(a, core * half, half, a.ndim - 1)
     mixed = resid.astype(f32) + cols(vis_proj_bias)
@@ -463,21 +498,14 @@
     requests = owner.shape[0]
     merged = merged.reshape(requests, -1, half)
     outgoing = place(owner, merged, groups)
-    outgoing, x_other = after((outgoing, x_other))
-
     images = lax.all_to_all(outgoing, ("phase", "rep"), split_axis=0, concat_axis=0, tiled=True)
-    ways = jnp.stack(
-        [((chip - by) % chips) * 2 + side for side in (core, 1 - core) for by in (0, 1, -1, 2)]
-    ).astype(jnp.int32)
-    x, row_factor = ordered(ways, rows, (x_side, x_other))
 
     image_at = routes[:, 0] - 1
     page_at = lax.dynamic_slice_in_dim(routes, phase * n_rep, n_rep, 0)[:, 1 : 1 + CAP] - 1
     page_at = page_at.reshape(-1)
-    image_buffer = place(image_at, images, groups).reshape(-1, half)
     dest = (owners * CAP + page_iota - first_page).astype(jnp.int32)
-    weights, image_buffer, page_at, start, x, row_factor, dest = after(
-        (weights, image_buffer, page_at, start[:, None], x, row_factor, dest)
+    weights, outgoing, page_at, start, dest = after(
+        (weights, outgoing, page_at, start[:, None], dest)
     )
 
     kv, outgoing_pages = kv_rows(
@@ -487,8 +515,10 @@
     arrived_pages = lax.all_to_all(
         outgoing_pages.reshape(n_rep, CAP, page_rows, -1), "rep", split_axis=0, concat_axis=0, tiled=True
     )
+    (images,) = after((images,), kv)
+    image_buffer = place(image_at, images, groups).reshape(-1, half)
     attn_out = attend(x, weights, row_factor, b_query[None, :], cosine, sines, start, kv)
-    kv_pool = place(page_at, arrived_pages.reshape(n_rep * CAP, page_rows, -1), pages)
+    kv_pool = pool(page_at, arrived_pages.reshape(n_rep * CAP, page_rows, -1), pages)
     return (image_buffer, attn_out, kv_pool)
 
 

time: 192 us -> 201 us (1.047)
  Pallas kernels: 58.9 us -> 66.5 us
    all_to_all x1, waiting for transfers between devices: 15.2 us -> 0.01 us  [body(): lax.all_to_all(outgoing, ('phase', 'rep'), split_axis=0, concat_axis=0, t...]
    all_gather x1, waiting for transfers between devices: 10.6 us -> 22.6 us  [body(): weights = lax.all_gather(own, ('phase', 'rep'), axis=0, tiled=True)]
    pallas_call x0 -> x1, Pallas kernels: none -> 10.1 us  [pool(): pl.pallas_call(pool_kernel, in_specs=[pl.BlockSpec(memory_space=pltpu.SME...]
    ppermute x3, waiting for transfers between devices: 1.04 us -> 7.85 us  [body(): lax.ppermute(a, 'tp', [(i, i ^ 1) for i in range(tp_ways)])]
    pallas_call x3 -> x2, Pallas kernels: 8.42 us -> 5.87 us  [place(): pl.pallas_call(place_kernel, grid_spec=pltpu.PrefetchScalarGridSpec(num_s...]
    all_to_all x1, waiting for transfers between devices: 7.22 us -> 4.72 us  [body(): lax.all_to_all(outgoing_pages.reshape(n_rep, CAP, page_rows, -1), 'rep',...]
  transfers between devices with their start and end apart: 13 -> 13, of which waited for: 11 -> 10; matrix products, arithmetic and copies ran while one was open for 9% -> 8% of each run, Pallas kernels for 24% -> 27%
where the time goes in v2:
time: 201 us; the launch traced here: 199 us
  Pallas kernels  66.5 us (33%)
  waiting for transfers between devices  62.2 us (31%)
  starting transfers between devices  36.8 us (18%)
  between operations  14.3 us (7%)
  local copies, waits for them, and re-layouts  10.6 us (5%)
  other arithmetic  8.67 us (4%)
    all_gather x1, waiting for transfers between devices, body(): weights = lax.all_gather(own, ('phase', 'rep'), axis=0, tiled=True)  22.6 us
    ppermute x6, waiting for transfers between devices, body(): lax.ppermute(a, 'tp', [(i, (i + 2 * by) % tp_ways) for i in range(tp_ways)])  21.1 us
    pallas_call x1, Pallas kernels, vision_partial(): pl.pallas_call(vision_kernel, grid_spec=pltpu.PrefetchScalarGridSpec(num_...  14.4 us
    all_to_all x1, starting transfers between devices, body(): lax.all_to_all(jnp.concatenate([to_images, to_pages], axis=1), ('phase',...  11.6 us
    pallas_call x1, Pallas kernels, attend(): pl.pallas_call(attend_kernel, in_specs=[anywhere()] * 2 + [resident()] *...  11.6 us
    all_to_all x1, starting transfers between devices, body(): lax.all_to_all(outgoing, ('phase', 'rep'), split_axis=0, concat_axis=0, t...  11.1 us
    pallas_call x1, Pallas kernels, pool(): pl.pallas_call(pool_kernel, in_specs=[pl.BlockSpec(memory_space=pltpu.SME...  10.1 us
    ppermute x6, starting transfers between devices, body(): lax.ppermute(a, 'tp', [(i, (i + 2 * by) % tp_ways) for i in range(tp_ways)])  9.04 us
  transfers between devices with their start and end apart: 13, of which 10 were waited for; matrix products, arithmetic and copies ran while one was open for 8% of the time, Pallas kernels for 27%

profile of v2, /device:TPU:2, one launch (start us, length us, event | category | flops | bytes accessed | tf_op | source)
XLA Modules:
  0.0 199.0 jit_solution(5649053987219412235)
XLA Ops:
  7.3 0.8 dynamic_slice.31
  8.0 0.8 copy.37.gain_ref
  8.8 1.9 shard_map.215
  10.8 1.6 collective-permute-start
  12.3 0.9 collective-permute-start.1
  13.2 0.5 broadcast.115
  13.7 0.7 reduce.5
  14.5 2.7 %copy.35.order_ref = s32[4,256,1]{2,1,0:T(8,128)} copy(s32[4,256,1]{0,1,2:T(8,128)S(1)} %bitcast.59) | data formatting | bytes 8192 | tf_op jit(solution)/shard_map/broadcast_in_dim | solution.py:438
  17.3 0.6 copy.43
  17.9 0.6 pad_add_fusion.1.own_ref
  18.7 0.6 add_subtract_fusion
  19.4 14.4 %shard_map.211 = (bf16[4,256,640]{2,1,0:T(8,128)(2,1)}, bf16[4,256,640]{2,1,0:T(8,128)(2,1)}, bf16[256,640]{1,0:T(8,128)(2,1)}) custom-call(s32[2]{0:T(128)} %pad_add_fusion.1.own_ref, s32[4,256,1]{2,1,0:T(8,128)} %copy.35.order_ref, bf16[1024,1280]{1,0:T(8,128)(2,1)} %patches_ref.1, f32[1280]{0:T(1024)} %gain_ref.1, bf16[480,1280]{1,0:T(8,128)(2,1)} %bitcast.70, ...), custom_call_target="tpu_custom_call" | custom-call | flops 14000000000 | bytes 6000000 | tf_op jit(solution)/shard_map/pallas_call | solution.py:99
  33.7 2.2 %collective-permute-done.refs_1_ = bf16[512,1024]{1,0:T(8,128)(2,1)S(1)} collective-permute-done((bf16[512,1024]{1,0:T(8,128)(2,1)}, bf16[512,1024]{1,0:T(8,128)(2,1)S(1)}, u32[]{:S(2)}, u32[]{:S(2)}) %collective-permute-start) | collective-permute-done | bytes 1048608 | tf_op jit(solution)/shard_map/ppermute | solution.py:421
  36.0 1.3 collective-permute-done.1.refs_2_
  37.6 2.3 %collective-permute-start.3 = (bf16[512,1024]{1,0:T(8,128)(2,1)}, bf16[512,1024]{1,0:T(8,128)(2,1)}, u32[]{:S(2)}, u32[]{:S(2)}) collective-permute-start(bf16[512,1024]{1,0:T(8,128)(2,1)} %refs_0_), channel_id=1, source_target_pairs={{0,4},{1,5},{2,6},{3,7},{4,0},{5,1},{6,2},{7,3},{8,12},{9,13},{10,... | collective-permute-start | bytes 3145736 | tf_op jit(solution)/shard_map/ppermute | solution.py:421
  39.9 0.7 copy.36
  40.6 11.6 %all-to-all-start = ((s32[32,1,8]{2,1,0:T(1,128)}), s32[32,1,8]{2,1,0:T(1,128)S(1)}, u32[]{:S(2)}, u32[]{:S(2)}) async-start(s32[32,1,8]{2,1,0:T(1,128)} %bitcast.10), calls=%async_computation | async-start | bytes 32768 | tf_op jit(solution)/shard_map/all_to_all | solution.py:465
  52.3 1.0 fusion.3
  53.3 1.0 pad_maximum_fusion
  54.4 1.6 add_convert_fusion
  56.0 5.9 %all-to-all-done = s32[32,1,8]{2,1,0:T(1,128)S(1)} async-done(((s32[32,1,8]{2,1,0:T(1,128)}), s32[32,1,8]{2,1,0:T(1,128)S(1)}, u32[]{:S(2)}, u32[]{:S(2)}) %all-to-all-start) | async-done | bytes 1056 | tf_op jit(solution)/shard_map/all_to_all | solution.py:465
  61.9 3.2 %collective-permute-done.3.refs_3_ = bf16[512,1024]{1,0:T(8,128)(2,1)} collective-permute-done((bf16[512,1024]{1,0:T(8,128)(2,1)}, bf16[512,1024]{1,0:T(8,128)(2,1)}, u32[]{:S(2)}, u32[]{:S(2)}) %collective-permute-start.3) | collective-permute-done | bytes 1048608 | tf_op jit(solution)/shard_map/ppermute | solution.py:421
  65.0 5.0 %shard_map.212.refs_0_ = bf16[2048,1024]{1,0:T(8,128)(2,1)} custom-call(bf16[512,1024]{1,0:T(8,128)(2,1)} %refs_0_, bf16[512,1024]{1,0:T(8,128)(2,1)} %copy-done.4, bf16[512,1024]{1,0:T(8,128)(2,1)} %collective-permute-done.1.refs_2_, bf16[512,1024]{1,0:T(8,128)(2,1)} %collective-permute-done.3.refs_3_), custom_call_target="tpu_custom_call" | custom-call | tf_op jit(solution)/shard_map/pallas_call | solution.py:138
  70.1 0.7 stack.47.ways_ref
  70.8 6.8 %collective-permute-done.4.refs_1_ = bf16[2048,1024]{1,0:T(8,128)(2,1)} collective-permute-done((bf16[2048,1024]{1,0:T(8,128)(2,1)}, bf16[2048,1024]{1,0:T(8,128)(2,1)}, u32[]{:S(2)}, u32[]{:S(2)}) %collective-permute-start.4) | collective-permute-done | bytes 4194336 | tf_op jit(solution)/shard_map/ppermute | solution.py:424
  77.6 8.7 %shard_map.213 = (bf16[8,512,1024]{2,1,0:T(8,128)(2,1)}, f32[512,1]{1,0:T(8,128)}) custom-call(s32[8]{0:T(128)} %stack.47.ways_ref, bf16[2048,1024]{1,0:T(8,128)(2,1)} %shard_map.212.refs_0_, bf16[2048,1024]{1,0:T(8,128)(2,1)} %collective-permute-done.4.refs_1_), custom_call_target="tpu_custom_call" | custom-call | flops 1000000 | bytes 1000 | tf_op jit(solution)/shard_map/pallas_call | solution.py:267
  86.3 0.8 dynamic-slice_bitcast_fusion.2
  87.1 1.1 collective-permute-start.5
  88.2 1.0 collective-permute-start.6
  89.1 2.3 %collective-permute-start.7 = (bf16[256,640]{1,0:T(8,128)(2,1)S(1)}, bf16[256,640]{1,0:T(8,128)(2,1)S(1)}, u32[]{:S(2)}, u32[]{:S(2)}) collective-permute-start(bf16[256,640]{1,0:T(8,128)(2,1)S(1)} %get-tuple-element.58), channel_id=1, source_target_pairs={{0,4},{1,5},{2,6},{3,7},{4,0},{5,1},{6,2},{7,3},{8,12},{9,13},{10,... | collective-permute-start | bytes 983048 | tf_op jit(solution)/shard_map/ppermute | solution.py:421
  91.5 6.4 %collective-permute-done.5 = bf16[256,640]{1,0:T(8,128)(2,1)S(1)} collective-permute-done((bf16[256,640]{1,0:T(8,128)(2,1)}, bf16[256,640]{1,0:T(8,128)(2,1)S(1)}, u32[]{:S(2)}, u32[]{:S(2)}) %collective-permute-start.5) | collective-permute-done | bytes 327712 | tf_op jit(solution)/shard_map/ppermute | solution.py:421
  97.9 8.0 %collective-permute-done.7 = bf16[256,640]{1,0:T(8,128)(2,1)S(1)} collective-permute-done((bf16[256,640]{1,0:T(8,128)(2,1)S(1)}, bf16[256,640]{1,0:T(8,128)(2,1)S(1)}, u32[]{:S(2)}, u32[]{:S(2)}) %collective-permute-start.7) | collective-permute-done | bytes 327712 | tf_op jit(solution)/shard_map/ppermute | solution.py:421
  106.4 1.0 collective-permute-done.8
  107.4 1.0 multiply_convert_fusion
  108.4 2.8 %shard_map.214 = bf16[32,16,640]{2,1,0:T(8,128)(2,1)} custom-call(s32[16]{0:T(128)} %bitcast.66, bf16[16,16,640]{2,1,0:T(8,128)(2,1)} %bitcast.56), custom_call_target="tpu_custom_call" | custom-call | tf_op jit(solution)/shard_map/pallas_call | solution.py:183
  111.2 11.1 %all-to-all-start.1 = ((bf16[32,16,640]{2,1,0:T(8,128)(2,1)}), bf16[32,16,640]{2,1,0:T(8,128)(2,1)S(1)}, u32[]{:S(2)}, u32[]{:S(2)}) async-start(bf16[32,16,640]{2,1,0:T(8,128)(2,1)} %shard_map.214), calls=%async_computation.1 | async-start | bytes 1310720 | tf_op jit(solution)/shard_map/all_to_all | solution.py:501
  122.4 0.6 pad_maximum_fusion.2
  123.1 0.7 reshape.148.at_ref
  123.7 0.6 add_reduce_fusion.at_ref
  124.4 22.6 %all-gather.2.cloned.1.call-done.w_ref = bf16[8192,768]{1,0:T(8,128)(2,1)} async-done(((bf16[256,768]{1,0:T(8,128)(2,1)}), bf16[8192,768]{1,0:T(8,128)(2,1)}) %all-gather.2.cloned.1.call-update) | async-done | bytes 12582928 | tf_op jit(solution)/shard_map/all_gather | solution.py:433
  147.0 0.9 copy.38.refs_4_
  147.8 9.0 %shard_map.216 = (bf16[512,256]{1,0:T(8,128)(2,1)}, bf16[40,32,256]{2,1,0:T(8,128)(2,1)}) custom-call(s32[16]{0:T(128)} %get-tuple-element.46.dest_ref, bf16[8,512,1024]{2,1,0:T(8,128)(2,1)} %get-tuple-element.47.x_ref, bf16[8192,768]{1,0:T(8,128)(2,1)} %all-gather.2.cloned.1.call-done.w_ref, f32[512,1]{1,0:T(8,128)} %get-tuple-element.49.refs_0_, ...), custom_call_target="tpu_custom_call" | custom-call | flops 7000000000 | bytes 13000000 | tf_op jit(solution)/shard_map/pallas_call | solution.py:319
  156.9 4.9 %all-to-all-start.2 = ((bf16[8,5,32,256]{3,2,1,0:T(8,128)(2,1)}), bf16[8,5,32,256]{3,2,1,0:T(8,128)(2,1)S(1)}, u32[]{:S(2)}, u32[]{:S(2)}) async-start(bf16[8,5,32,256]{3,2,1,0:T(8,128)(2,1)} %bitcast.58), calls=%async_computation.2 | async-start | bytes 1310720 | tf_op jit(solution)/shard_map/all_to_all | solution.py:515
  161.8 3.1 %shard_map.217 = bf16[32,16,640]{2,1,0:T(8,128)(2,1)} custom-call(s32[32]{0:T(128)} %add_reduce_fusion.at_ref, bf16[32,16,640]{2,1,0:T(8,128)(2,1)} %copy-done), custom_call_target="tpu_custom_call" | custom-call | tf_op jit(solution)/shard_map/pallas_call | solution.py:183
  164.9 11.6 %shard_map.218 = bf16[512,512]{1,0:T(8,128)(2,1)} custom-call(bf16[8,512,1024]{2,1,0:T(8,128)(2,1)} %get-tuple-element.47.x_ref, bf16[8192,768]{1,0:T(8,128)(2,1)} %all-gather.2.cloned.1.call-done.w_ref, f32[512,1]{1,0:T(8,128)} %get-tuple-element.49.refs_0_, f32[1,512]{1,0:T(1,128)} %bitcast.71, f32[512,128]{1,0:T(8,128)} %get-tuple-element.50.refs_2_, ...), custom_call_target="tpu_custom_call" | custom-call | flops 14000000000 | bytes 17000000 | tf_op jit(solution)/shard_map/pallas_call | solution.py:386
  176.5 4.7 %all-to-all-done.2 = bf16[8,5,32,256]{3,2,1,0:T(8,128)(2,1)S(1)} async-done(((bf16[8,5,32,256]{3,2,1,0:T(8,128)(2,1)}), bf16[8,5,32,256]{3,2,1,0:T(8,128)(2,1)S(1)}, u32[]{:S(2)}, u32[]{:S(2)}) %all-to-all-start.2) | async-done | bytes 655392 | tf_op jit(solution)/shard_map/all_to_all | solution.py:515
  181.2 0.9 copy-done.1
  182.1 10.1 %shard_map.219 = bf16[16,32,256]{2,1,0:T(8,128)(2,1)} custom-call(s32[40]{0:T(128)} %reshape.148.at_ref, bf16[40,32,256]{2,1,0:T(8,128)(2,1)} %bitcast.55), custom_call_target="tpu_custom_call" | custom-call | tf_op jit(solution)/shard_map/pallas_call | solution.py:216
  (59 shorter events, 1.7 us)
Async XLA Ops:
  7.2 6.6 %copy-start.5 = (s32[1,1024]{1,0:T(1,128)S(1)}, s32[1,1024]{1,0:T(1,128)}, u32[]{:S(2)}) copy-start(s32[1,1024]{1,0:T(1,128)} %param.21) | copy-start | bytes 12292
  7.2 10.0 %copy-start.6 = (f32[480]{0:T(512)S(1)}, f32[480]{0:T(512)}, u32[]{:S(2)}) copy-start(f32[480]{0:T(512)} %param.24) | copy-start | bytes 5764
  7.2 11.4 %copy-start.10 = (s32[1,16]{1,0:T(1,128)S(1)}, s32[1,16]{1,0:T(1,128)}, u32[]{:S(2)}) copy-start(s32[1,16]{1,0:T(1,128)} %param.38) | copy-start | bytes 196
  7.2 11.5 %copy-start.13 = (s32[1,16]{1,0:T(1,128)S(1)}, s32[1,16]{1,0:T(1,128)}, u32[]{:S(2)}) copy-start(s32[1,16]{1,0:T(1,128)} %param.39) | copy-start | bytes 196
  7.2 139.8 %all-gather.2.cloned.1.call-start = ((), (), s32[]{:S(2)}) async-start(), calls=%async_computation.3 | async-start | bytes 12976128 | tf_op jit(solution)/shard_map/all_gather | solution.py:433
  10.8 25.2 %collective-permute-start = (bf16[512,1024]{1,0:T(8,128)(2,1)}, bf16[512,1024]{1,0:T(8,128)(2,1)S(1)}, u32[]{:S(2)}, u32[]{:S(2)}) collective-permute-start(bf16[512,1024]{1,0:T(8,128)(2,1)} %refs_0_), channel_id=1, source_target_pairs={{0,2},{1,3},{2,4},{3,5},{4,6},{5,7},{6,0},{7,1},{8,10},{9,11},{10,... | collective-permute-start | bytes 3145736 | tf_op jit(solution)/shard_map/ppermute | solution.py:421
  12.3 24.9 %collective-permute-start.1 = (bf16[512,1024]{1,0:T(8,128)(2,1)}, bf16[512,1024]{1,0:T(8,128)(2,1)}, u32[]{:S(2)}, u32[]{:S(2)}) collective-permute-start(bf16[512,1024]{1,0:T(8,128)(2,1)} %refs_0_), channel_id=1, source_target_pairs={{0,6},{1,7},{2,0},{3,1},{4,2},{5,3},{6,4},{7,5},{8,14},{9,15},{10,... | collective-permute-start | bytes 3145736 | tf_op jit(solution)/shard_map/ppermute | solution.py:421
  19.3 17.9 %copy-start.14 = (s32[1,16]{1,0:T(1,128)S(1)}, s32[1,16]{1,0:T(1,128)}, u32[]{:S(2)}) copy-start(s32[1,16]{1,0:T(1,128)} %param.29) | copy-start | bytes 196
  19.4 17.9 %copy-start.9 = (s32[1,16]{1,0:T(1,128)S(1)}, s32[1,16]{1,0:T(1,128)}, u32[]{:S(2)}) copy-start(s32[1,16]{1,0:T(1,128)} %param.28) | copy-start | bytes 196
  33.7 20.7 %copy-start.2 = (bf16[4,256,640]{2,1,0:T(8,128)(2,1)S(1)}, bf16[4,256,640]{2,1,0:T(8,128)(2,1)}, u32[]{:S(2)}) copy-start(bf16[4,256,640]{2,1,0:T(8,128)(2,1)} %get-tuple-element.33) | copy-start | bytes 3932164
  36.0 18.4 %copy-start.4 = (bf16[512,1024]{1,0:T(8,128)(2,1)}, bf16[512,1024]{1,0:T(8,128)(2,1)S(1)}, u32[]{:S(2)}) copy-start(bf16[512,1024]{1,0:T(8,128)(2,1)S(1)} %collective-permute-done.refs_1_) | copy-start | bytes 3145732
  37.3 17.1 %collective-permute-start.2 = (bf16[4,256,640]{2,1,0:T(8,128)(2,1)}, bf16[4,256,640]{2,1,0:T(8,128)(2,1)}, u32[]{:S(2)}, u32[]{:S(2)}) collective-permute-start(bf16[4,256,640]{2,1,0:T(8,128)(2,1)} %get-tuple-element.34), channel_id=1, source_target_pairs={{0,1},{1,0},{2,3},{3,2},{4,5},{5,4},{6,7},{7,6},{8,9},{9,8},{10,11... | collective-permute-start | bytes 3932168 | tf_op jit(solution)/shard_map/ppermute | solution.py:424
  37.6 27.5 %collective-permute-start.3 = (bf16[512,1024]{1,0:T(8,128)(2,1)}, bf16[512,1024]{1,0:T(8,128)(2,1)}, u32[]{:S(2)}, u32[]{:S(2)}) collective-permute-start(bf16[512,1024]{1,0:T(8,128)(2,1)} %refs_0_), channel_id=1, source_target_pairs={{0,4},{1,5},{2,6},{3,7},{4,0},{5,1},{6,2},{7,3},{8,12},{9,13},{10,... | collective-permute-start | bytes 3145736 | tf_op jit(solution)/shard_map/ppermute | solution.py:421
  40.6 21.3 %all-to-all-start = ((s32[32,1,8]{2,1,0:T(1,128)}), s32[32,1,8]{2,1,0:T(1,128)S(1)}, u32[]{:S(2)}, u32[]{:S(2)}) async-start(s32[32,1,8]{2,1,0:T(1,128)} %bitcast.10), calls=%async_computation | async-start | bytes 32768 | tf_op jit(solution)/shard_map/all_to_all | solution.py:465
  70.1 7.5 %collective-permute-start.4 = (bf16[2048,1024]{1,0:T(8,128)(2,1)}, bf16[2048,1024]{1,0:T(8,128)(2,1)}, u32[]{:S(2)}, u32[]{:S(2)}) collective-permute-start(bf16[2048,1024]{1,0:T(8,128)(2,1)} %shard_map.212.refs_0_), channel_id=1, source_target_pairs={{0,1},{1,0},{2,3},{3,2},{4,5},{5,4},{6,7},{7,6},{8,9},{9,8},{10,11... | collective-permute-start | bytes 12582920 | tf_op jit(solution)/shard_map/ppermute | solution.py:424
  86.2 5.2 %copy-start.7 = (f32[1280]{0:T(1024)S(1)}, f32[1280]{0:T(1024)}, u32[]{:S(2)}) copy-start(f32[1280]{0:T(1024)} %param.26) | copy-start | bytes 15364
  86.3 19.6 %copy-start.3 = (bf16[256,640]{1,0:T(8,128)(2,1)S(1)}, bf16[256,640]{1,0:T(8,128)(2,1)}, u32[]{:S(2)}) copy-start(bf16[256,640]{1,0:T(8,128)(2,1)} %get-tuple-element.37) | copy-start | bytes 983044
  87.1 19.2 %copy-start.8 = (f32[1280]{0:T(1024)S(1)}, f32[1280]{0:T(1024)}, u32[]{:S(2)}) copy-start(f32[1280]{0:T(1024)} %param.27) | copy-start | bytes 15364
  87.1 10.8 %collective-permute-start.5 = (bf16[256,640]{1,0:T(8,128)(2,1)}, bf16[256,640]{1,0:T(8,128)(2,1)S(1)}, u32[]{:S(2)}, u32[]{:S(2)}) collective-permute-start(bf16[256,640]{1,0:T(8,128)(2,1)} %get-tuple-element.57), channel_id=1, source_target_pairs={{0,2},{1,3},{2,4},{3,5},{4,6},{5,7},{6,0},{7,1},{8,10},{9,11},{10,... | collective-permute-start | bytes 983048 | tf_op jit(solution)/shard_map/ppermute | solution.py:421
  88.2 9.7 %collective-permute-start.6 = (bf16[256,640]{1,0:T(8,128)(2,1)S(1)}, bf16[256,640]{1,0:T(8,128)(2,1)S(1)}, u32[]{:S(2)}, u32[]{:S(2)}) collective-permute-start(bf16[256,640]{1,0:T(8,128)(2,1)S(1)} %get-tuple-element.59), channel_id=1, source_target_pairs={{0,6},{1,7},{2,0},{3,1},{4,2},{5,3},{6,4},{7,5},{8,14},{9,15},{10,... | collective-permute-start | bytes 983048 | tf_op jit(solution)/shard_map/ppermute | solution.py:421
  89.1 16.8 %collective-permute-start.7 = (bf16[256,640]{1,0:T(8,128)(2,1)S(1)}, bf16[256,640]{1,0:T(8,128)(2,1)S(1)}, u32[]{:S(2)}, u32[]{:S(2)}) collective-permute-start(bf16[256,640]{1,0:T(8,128)(2,1)S(1)} %get-tuple-element.58), channel_id=1, source_target_pairs={{0,4},{1,5},{2,6},{3,7},{4,0},{5,1},{6,2},{7,3},{8,12},{9,13},{10,... | collective-permute-start | bytes 983048 | tf_op jit(solution)/shard_map/ppermute | solution.py:421
  106.2 1.2 collective-permute-start.8
  108.4 14.0 %copy-start.11 = (f32[128]{0:T(128)S(1)}, f32[128]{0:T(128)}, u32[]{:S(2)}) copy-start(f32[128]{0:T(128)} %param.37) | copy-start | bytes 1540
  108.4 14.0 %copy-start.12 = (f32[128]{0:T(128)S(1)}, f32[128]{0:T(128)}, u32[]{:S(2)}) copy-start(f32[128]{0:T(128)} %param.35) | copy-start | bytes 1540
  111.2 45.6 %all-to-all-start.1 = ((bf16[32,16,640]{2,1,0:T(8,128)(2,1)}), bf16[32,16,640]{2,1,0:T(8,128)(2,1)S(1)}, u32[]{:S(2)}, u32[]{:S(2)}) async-start(bf16[32,16,640]{2,1,0:T(8,128)(2,1)} %shard_map.214), calls=%async_computation.1 | async-start | bytes 1310720 | tf_op jit(solution)/shard_map/all_to_all | solution.py:501
  156.9 4.9 %copy-start = (bf16[32,16,640]{2,1,0:T(8,128)(2,1)}, bf16[32,16,640]{2,1,0:T(8,128)(2,1)S(1)}, u32[]{:S(2)}) copy-start(bf16[32,16,640]{2,1,0:T(8,128)(2,1)S(1)} %all-to-all-done.1.items_ref) | copy-start | bytes 1966084
  156.9 24.3 %all-to-all-start.2 = ((bf16[8,5,32,256]{3,2,1,0:T(8,128)(2,1)}), bf16[8,5,32,256]{3,2,1,0:T(8,128)(2,1)S(1)}, u32[]{:S(2)}, u32[]{:S(2)}) async-start(bf16[8,5,32,256]{3,2,1,0:T(8,128)(2,1)} %bitcast.58), calls=%async_computation.2 | async-start | bytes 1310720 | tf_op jit(solution)/shard_map/all_to_all | solution.py:515
  181.2 0.9 copy-start.1
Sparse Core Ops, SparseCore 0:
  10.9 136.0 all-gather.1

commit v3 on v1

--- a/solution.py
+++ b/solution.py
@@ -448,9 +448,14 @@
         (chip_sum, x_far, x_own, routes, cosine, sines)
     )
 
+    x_side = join(x_own, *x_near, x_far)
+    ways = jnp.stack(
+        [((chip - by) % chips) * 2 + side for side in (core, 1 - core) for by in (0, 1, -1, 2)]
+    ).astype(jnp.int32)
+    x, row_factor = ordered(ways, rows, (x_side, partner(x_side)))
+    chip_sum, x, row_factor = after((chip_sum, x, row_factor))
+
     arrived = [across(take(chip_sum, (chip + by) % chips), by) for by in (1, -1, 2)]
-    x_side = join(x_own, *x_near, x_far)
-    x_other = partner(x_side)
     half = width // 2
     cols = lambda a: lax.dynamic_slice_in_dim(a, core * half, half, a.ndim - 1)
     mixed = resid.astype(f32) + cols(vis_proj_bias)
@@ -463,23 +468,15 @@
     requests = owner.shape[0]
     merged = merged.reshape(requests, -1, half)
     outgoing = place(owner, merged, groups)
-    outgoing, x_other = after((outgoing, x_other))
-
-    images = lax.all_to_all(outgoing, ("phase", "rep"), split_axis=0, concat_axis=0, tiled=True)
-    ways = jnp.stack(
-        [((chip - by) % chips) * 2 + side for side in (core, 1 - core) for by in (0, 1, -1, 2)]
-    ).astype(jnp.int32)
-    x, row_factor = ordered(ways, rows, (x_side, x_other))
-
     image_at = routes[:, 0] - 1
     page_at = lax.dynamic_slice_in_dim(routes, phase * n_rep, n_rep, 0)[:, 1 : 1 + CAP] - 1
     page_at = page_at.reshape(-1)
-    image_buffer = place(image_at, images, groups).reshape(-1, half)
     dest = (owners * CAP + page_iota - first_page).astype(jnp.int32)
-    weights, image_buffer, page_at, start, x, row_factor, dest = after(
-        (weights, image_buffer, page_at, start[:, None], x, row_factor, dest)
-    )
-
+    weights, outgoing, page_at, start, dest = after(
+        (weights, outgoing, page_at, start[:, None], dest)
+    )
+
+    images = lax.all_to_all(outgoing, ("phase", "rep"), split_axis=0, concat_axis=0, tiled=True)
     kv, outgoing_pages = kv_rows(
         dest, x, weights, row_factor, jnp.concatenate([b_key, b_value])[None, :], cosine, sines,
         n_rep * CAP, page_rows,
@@ -487,6 +484,8 @@
     arrived_pages = lax.all_to_all(
         outgoing_pages.reshape(n_rep, CAP, page_rows, -1), "rep", split_axis=0, concat_axis=0, tiled=True
     )
+    (images,) = after((images,), kv)
+    image_buffer = place(image_at, images, groups).reshape(-1, half)
     attn_out = attend(x, weights, row_factor, b_query[None, :], cosine, sines, start, kv)
     kv_pool = place(page_at, arrived_pages.reshape(n_rep * CAP, page_rows, -1), pages)
     return (image_buffer, attn_out, kv_pool)

time: 192 us -> 203 us (1.057)
  waiting for transfers between devices: 61.4 us -> 80 us
  starting transfers between devices: 36.5 us -> 29.3 us
    all_gather x1, waiting for transfers between devices: 10.6 us -> 22.5 us  [body(): weights = lax.all_gather(own, ('phase', 'rep'), axis=0, tiled=True)]
    all_to_all x1, waiting for transfers between devices: 7.22 us -> 18.4 us  [body(): lax.all_to_all(outgoing_pages.reshape(n_rep, CAP, page_rows, -1), 'rep',...]
    all_to_all x1, waiting for transfers between devices: 15.2 us -> 5.63 us  [body(): lax.all_to_all(outgoing, ('phase', 'rep'), split_axis=0, concat_axis=0, t...]
    all_to_all x1, starting transfers between devices: 11.2 us -> 4.12 us  [body(): lax.all_to_all(outgoing, ('phase', 'rep'), split_axis=0, concat_axis=0, t...]
    ppermute x3, waiting for transfers between devices: 1.04 us -> 7.26 us  [body(): lax.ppermute(a, 'tp', [(i, i ^ 1) for i in range(tp_ways)])]
  transfers between devices with their start and end apart: 13 -> 13, of which waited for: 11 -> 11; matrix products, arithmetic and copies ran while one was open for 9% -> 8% of each run, Pallas kernels for 24% -> 22%
where the time goes in v3:
time: 203 us; the launch traced here: 202 us
  waiting for transfers between devices  80 us (39%)
  Pallas kernels  58.8 us (29%)
  starting transfers between devices  29.3 us (14%)
  between operations  14.3 us (7%)
  local copies, waits for them, and re-layouts  10.6 us (5%)
  other arithmetic  8.65 us (4%)
    all_gather x1, waiting for transfers between devices, body(): weights = lax.all_gather(own, ('phase', 'rep'), axis=0, tiled=True)  22.5 us
    ppermute x6, waiting for transfers between devices, body(): lax.ppermute(a, 'tp', [(i, (i + 2 * by) % tp_ways) for i in range(tp_ways)])  20.4 us
    all_to_all x1, waiting for transfers between devices, body(): lax.all_to_all(outgoing_pages.reshape(n_rep, CAP, page_rows, -1), 'rep',...  18.4 us
    pallas_call x1, Pallas kernels, vision_partial(): pl.pallas_call(vision_kernel, grid_spec=pltpu.PrefetchScalarGridSpec(num_...  14.4 us
    all_to_all x1, starting transfers between devices, body(): lax.all_to_all(jnp.concatenate([to_images, to_pages], axis=1), ('phase',...  11.6 us
    pallas_call x1, Pallas kernels, attend(): pl.pallas_call(attend_kernel, in_specs=[anywhere()] * 2 + [resident()] *...  11.6 us
    ppermute x6, starting transfers between devices, body(): lax.ppermute(a, 'tp', [(i, (i + 2 * by) % tp_ways) for i in range(tp_ways)])  9.04 us
    pallas_call x1, Pallas kernels, kv_rows(): pl.pallas_call(kv_kernel, in_specs=[pl.BlockSpec(memory_space=pltpu.SMEM)...  8.99 us
  transfers between devices with their start and end apart: 13, of which 11 were waited for; matrix products, arithmetic and copies ran while one was open for 8% of the time, Pallas kernels for 22%

profile of v3, /device:TPU:2, one launch (start us, length us, event | category | flops | bytes accessed | tf_op | source)
XLA Modules:
  0.0 201.6 jit_solution(17343752627144776234)
XLA Ops:
  7.3 0.8 dynamic_slice.25
  8.0 0.8 copy.37.gain_ref
  8.8 1.9 shard_map.212
  10.8 1.6 collective-permute-start
  12.3 0.9 collective-permute-start.1
  13.2 0.5 broadcast.115
  13.7 0.7 reduce.5
  14.5 2.7 %copy.35.order_ref = s32[4,256,1]{2,1,0:T(8,128)} copy(s32[4,256,1]{0,1,2:T(8,128)S(1)} %bitcast.59) | data formatting | bytes 8192 | tf_op jit(solution)/shard_map/broadcast_in_dim | solution.py:408
  17.3 0.6 copy.43
  17.9 0.6 pad_add_fusion.1.own_ref
  18.7 0.6 add_subtract_fusion
  19.4 14.4 %shard_map.211 = (bf16[4,256,640]{2,1,0:T(8,128)(2,1)}, bf16[4,256,640]{2,1,0:T(8,128)(2,1)}, bf16[256,640]{1,0:T(8,128)(2,1)}) custom-call(s32[2]{0:T(128)} %pad_add_fusion.1.own_ref, s32[4,256,1]{2,1,0:T(8,128)} %copy.35.order_ref, bf16[1024,1280]{1,0:T(8,128)(2,1)} %patches_ref.1, f32[1280]{0:T(1024)} %gain_ref.1, bf16[480,1280]{1,0:T(8,128)(2,1)} %bitcast.70, ...), custom_call_target="tpu_custom_call" | custom-call | flops 14000000000 | bytes 6000000 | tf_op jit(solution)/shard_map/pallas_call | solution.py:99
  33.7 2.2 %collective-permute-done.refs_1_ = bf16[512,1024]{1,0:T(8,128)(2,1)S(1)} collective-permute-done((bf16[512,1024]{1,0:T(8,128)(2,1)}, bf16[512,1024]{1,0:T(8,128)(2,1)S(1)}, u32[]{:S(2)}, u32[]{:S(2)}) %collective-permute-start) | collective-permute-done | bytes 1048608 | tf_op jit(solution)/shard_map/ppermute | solution.py:391
  36.0 1.3 collective-permute-done.1.refs_2_
  37.6 2.3 %collective-permute-start.3 = (bf16[512,1024]{1,0:T(8,128)(2,1)}, bf16[512,1024]{1,0:T(8,128)(2,1)}, u32[]{:S(2)}, u32[]{:S(2)}) collective-permute-start(bf16[512,1024]{1,0:T(8,128)(2,1)} %refs_0_), channel_id=1, source_target_pairs={{0,4},{1,5},{2,6},{3,7},{4,0},{5,1},{6,2},{7,3},{8,12},{9,13},{10,... | collective-permute-start | bytes 3145736 | tf_op jit(solution)/shard_map/ppermute | solution.py:391
  39.9 0.7 copy.36
  40.6 11.6 %all-to-all-start = ((s32[32,1,8]{2,1,0:T(1,128)}), s32[32,1,8]{2,1,0:T(1,128)S(1)}, u32[]{:S(2)}, u32[]{:S(2)}) async-start(s32[32,1,8]{2,1,0:T(1,128)} %bitcast.10), calls=%async_computation | async-start | bytes 32768 | tf_op jit(solution)/shard_map/all_to_all | solution.py:435
  52.3 1.0 fusion.3
  53.3 1.0 pad_maximum_fusion
  54.4 1.6 add_convert_fusion
  56.0 5.9 %all-to-all-done = s32[32,1,8]{2,1,0:T(1,128)S(1)} async-done(((s32[32,1,8]{2,1,0:T(1,128)}), s32[32,1,8]{2,1,0:T(1,128)S(1)}, u32[]{:S(2)}, u32[]{:S(2)}) %all-to-all-start) | async-done | bytes 1056 | tf_op jit(solution)/shard_map/all_to_all | solution.py:435
  61.9 3.2 %collective-permute-done.3.refs_3_ = bf16[512,1024]{1,0:T(8,128)(2,1)} collective-permute-done((bf16[512,1024]{1,0:T(8,128)(2,1)}, bf16[512,1024]{1,0:T(8,128)(2,1)}, u32[]{:S(2)}, u32[]{:S(2)}) %collective-permute-start.3) | collective-permute-done | bytes 1048608 | tf_op jit(solution)/shard_map/ppermute | solution.py:391
  65.0 5.0 %shard_map.213.refs_0_ = bf16[2048,1024]{1,0:T(8,128)(2,1)} custom-call(bf16[512,1024]{1,0:T(8,128)(2,1)} %refs_0_, bf16[512,1024]{1,0:T(8,128)(2,1)} %copy-done.4, bf16[512,1024]{1,0:T(8,128)(2,1)} %collective-permute-done.1.refs_2_, bf16[512,1024]{1,0:T(8,128)(2,1)} %collective-permute-done.3.refs_3_), custom_call_target="tpu_custom_call" | custom-call | tf_op jit(solution)/shard_map/pallas_call | solution.py:138
  70.1 0.7 stack.47.ways_ref
  70.8 6.8 %collective-permute-done.4.refs_1_ = bf16[2048,1024]{1,0:T(8,128)(2,1)} collective-permute-done((bf16[2048,1024]{1,0:T(8,128)(2,1)}, bf16[2048,1024]{1,0:T(8,128)(2,1)}, u32[]{:S(2)}, u32[]{:S(2)}) %collective-permute-start.4) | collective-permute-done | bytes 4194336 | tf_op jit(solution)/shard_map/ppermute | solution.py:394
  77.6 8.7 %shard_map.214 = (bf16[8,512,1024]{2,1,0:T(8,128)(2,1)}, f32[512,1]{1,0:T(8,128)}) custom-call(s32[8]{0:T(128)} %stack.47.ways_ref, bf16[2048,1024]{1,0:T(8,128)(2,1)} %shard_map.213.refs_0_, bf16[2048,1024]{1,0:T(8,128)(2,1)} %collective-permute-done.4.refs_1_), custom_call_target="tpu_custom_call" | custom-call | flops 1000000 | bytes 1000 | tf_op jit(solution)/shard_map/pallas_call | solution.py:237
  86.3 0.8 dynamic-slice_bitcast_fusion.2
  87.1 1.1 collective-permute-start.5
  88.2 1.0 collective-permute-start.6
  89.2 2.3 %collective-permute-start.7 = (bf16[256,640]{1,0:T(8,128)(2,1)S(1)}, bf16[256,640]{1,0:T(8,128)(2,1)S(1)}, u32[]{:S(2)}, u32[]{:S(2)}) collective-permute-start(bf16[256,640]{1,0:T(8,128)(2,1)S(1)} %get-tuple-element.60), channel_id=1, source_target_pairs={{0,4},{1,5},{2,6},{3,7},{4,0},{5,1},{6,2},{7,3},{8,12},{9,13},{10,... | collective-permute-start | bytes 983048 | tf_op jit(solution)/shard_map/ppermute | solution.py:391
  91.7 0.6 pad_maximum_fusion.2
  92.3 5.6 %collective-permute-done.5 = bf16[256,640]{1,0:T(8,128)(2,1)S(1)} collective-permute-done((bf16[256,640]{1,0:T(8,128)(2,1)}, bf16[256,640]{1,0:T(8,128)(2,1)S(1)}, u32[]{:S(2)}, u32[]{:S(2)}) %collective-permute-start.5) | collective-permute-done | bytes 327712 | tf_op jit(solution)/shard_map/ppermute | solution.py:391
  97.9 8.0 %collective-permute-done.7 = bf16[256,640]{1,0:T(8,128)(2,1)S(1)} collective-permute-done((bf16[256,640]{1,0:T(8,128)(2,1)S(1)}, bf16[256,640]{1,0:T(8,128)(2,1)S(1)}, u32[]{:S(2)}, u32[]{:S(2)}) %collective-permute-start.7) | collective-permute-done | bytes 327712 | tf_op jit(solution)/shard_map/ppermute | solution.py:391
  106.4 0.6 reshape.148.at_ref
  107.5 1.0 multiply_convert_fusion
  108.5 2.6 %shard_map.215 = bf16[32,16,640]{2,1,0:T(8,128)(2,1)} custom-call(s32[16]{0:T(128)} %bitcast.66, bf16[16,16,640]{2,1,0:T(8,128)(2,1)} %bitcast.56), custom_call_target="tpu_custom_call" | custom-call | tf_op jit(solution)/shard_map/pallas_call | solution.py:183
  111.1 22.5 %all-gather.2.cloned.1.call-done.w_ref = bf16[8192,768]{1,0:T(8,128)(2,1)} async-done(((bf16[256,768]{1,0:T(8,128)(2,1)}), bf16[8192,768]{1,0:T(8,128)(2,1)}) %all-gather.2.cloned.1.call-update) | async-done | bytes 12582928 | tf_op jit(solution)/shard_map/all_gather | solution.py:403
  133.6 9.0 %shard_map.216 = (bf16[512,256]{1,0:T(8,128)(2,1)}, bf16[40,32,256]{2,1,0:T(8,128)(2,1)}) custom-call(s32[16]{0:T(128)} %get-tuple-element.48.dest_ref, bf16[8,512,1024]{2,1,0:T(8,128)(2,1)} %get-tuple-element.49.x_ref, bf16[8192,768]{1,0:T(8,128)(2,1)} %all-gather.2.cloned.1.call-done.w_ref, f32[512,1]{1,0:T(8,128)} %get-tuple-element.51.refs_0_, ...), custom_call_target="tpu_custom_call" | custom-call | flops 7000000000 | bytes 13000000 | tf_op jit(solution)/shard_map/pallas_call | solution.py:289
  142.6 4.4 %all-to-all-start.2 = ((bf16[8,5,32,256]{3,2,1,0:T(8,128)(2,1)}), bf16[8,5,32,256]{3,2,1,0:T(8,128)(2,1)S(1)}, u32[]{:S(2)}, u32[]{:S(2)}) async-start(bf16[8,5,32,256]{3,2,1,0:T(8,128)(2,1)} %bitcast.58), calls=%async_computation.2 | async-start | bytes 1310720 | tf_op jit(solution)/shard_map/all_to_all | solution.py:484
  146.9 0.6 add_reduce_fusion.at_ref
  147.6 0.9 copy.38.refs_4_
  148.4 18.4 %all-to-all-done.2 = bf16[8,5,32,256]{3,2,1,0:T(8,128)(2,1)S(1)} async-done(((bf16[8,5,32,256]{3,2,1,0:T(8,128)(2,1)}), bf16[8,5,32,256]{3,2,1,0:T(8,128)(2,1)S(1)}, u32[]{:S(2)}, u32[]{:S(2)}) %all-to-all-start.2) | async-done | bytes 655392 | tf_op jit(solution)/shard_map/all_to_all | solution.py:484
  166.9 4.1 %all-to-all-start.1 = ((bf16[32,16,640]{2,1,0:T(8,128)(2,1)}), bf16[32,16,640]{2,1,0:T(8,128)(2,1)S(1)}, u32[]{:S(2)}, u32[]{:S(2)}) async-start(bf16[32,16,640]{2,1,0:T(8,128)(2,1)} %shard_map.215), calls=%async_computation.1 | async-start | bytes 1310720 | tf_op jit(solution)/shard_map/all_to_all | solution.py:479
  171.0 11.6 %shard_map.218 = bf16[512,512]{1,0:T(8,128)(2,1)} custom-call(bf16[8,512,1024]{2,1,0:T(8,128)(2,1)} %get-tuple-element.49.x_ref, bf16[8192,768]{1,0:T(8,128)(2,1)} %all-gather.2.cloned.1.call-done.w_ref, f32[512,1]{1,0:T(8,128)} %get-tuple-element.51.refs_0_, f32[1,512]{1,0:T(1,128)} %bitcast.71, f32[512,128]{1,0:T(8,128)} %get-tuple-element.52.refs_2_, ...), custom_call_target="tpu_custom_call" | custom-call | flops 14000000000 | bytes 17000000 | tf_op jit(solution)/shard_map/pallas_call | solution.py:356
  182.6 2.8 %shard_map.219 = bf16[16,32,256]{2,1,0:T(8,128)(2,1)} custom-call(s32[40]{0:T(128)} %reshape.148.at_ref, bf16[40,32,256]{2,1,0:T(8,128)(2,1)} %bitcast.55), custom_call_target="tpu_custom_call" | custom-call | tf_op jit(solution)/shard_map/pallas_call | solution.py:183
  185.4 5.6 %all-to-all-done.1.items_ref = bf16[32,16,640]{2,1,0:T(8,128)(2,1)S(1)} async-done(((bf16[32,16,640]{2,1,0:T(8,128)(2,1)}), bf16[32,16,640]{2,1,0:T(8,128)(2,1)S(1)}, u32[]{:S(2)}, u32[]{:S(2)}) %all-to-all-start.1) | async-done | bytes 655392 | tf_op jit(solution)/shard_map/all_to_all | solution.py:479
  191.0 0.9 copy-done.1
  191.9 2.9 %shard_map.217 = bf16[32,16,640]{2,1,0:T(8,128)(2,1)} custom-call(s32[32]{0:T(128)} %add_reduce_fusion.at_ref, bf16[32,16,640]{2,1,0:T(8,128)(2,1)} %copy-done.1), custom_call_target="tpu_custom_call" | custom-call | tf_op jit(solution)/shard_map/pallas_call | solution.py:183
  (59 shorter events, 2.2 us)
Async XLA Ops:
  7.2 6.6 %copy-start.5 = (s32[1,1024]{1,0:T(1,128)S(1)}, s32[1,1024]{1,0:T(1,128)}, u32[]{:S(2)}) copy-start(s32[1,1024]{1,0:T(1,128)} %param.21) | copy-start | bytes 12292
  7.2 10.0 %copy-start.6 = (f32[480]{0:T(512)S(1)}, f32[480]{0:T(512)}, u32[]{:S(2)}) copy-start(f32[480]{0:T(512)} %param.24) | copy-start | bytes 5764
  7.2 11.4 %copy-start.10 = (s32[1,16]{1,0:T(1,128)S(1)}, s32[1,16]{1,0:T(1,128)}, u32[]{:S(2)}) copy-start(s32[1,16]{1,0:T(1,128)} %param.38) | copy-start | bytes 196
  7.2 11.5 %copy-start.13 = (s32[1,16]{1,0:T(1,128)S(1)}, s32[1,16]{1,0:T(1,128)}, u32[]{:S(2)}) copy-start(s32[1,16]{1,0:T(1,128)} %param.39) | copy-start | bytes 196
  7.2 126.4 %all-gather.2.cloned.1.call-start = ((), (), s32[]{:S(2)}) async-start(), calls=%async_computation.3 | async-start | bytes 12976128 | tf_op jit(solution)/shard_map/all_gather | solution.py:403
  10.8 25.2 %collective-permute-start = (bf16[512,1024]{1,0:T(8,128)(2,1)}, bf16[512,1024]{1,0:T(8,128)(2,1)S(1)}, u32[]{:S(2)}, u32[]{:S(2)}) collective-permute-start(bf16[512,1024]{1,0:T(8,128)(2,1)} %refs_0_), channel_id=1, source_target_pairs={{0,2},{1,3},{2,4},{3,5},{4,6},{5,7},{6,0},{7,1},{8,10},{9,11},{10,... | collective-permute-start | bytes 3145736 | tf_op jit(solution)/shard_map/ppermute | solution.py:391
  12.3 24.9 %collective-permute-start.1 = (bf16[512,1024]{1,0:T(8,128)(2,1)}, bf16[512,1024]{1,0:T(8,128)(2,1)}, u32[]{:S(2)}, u32[]{:S(2)}) collective-permute-start(bf16[512,1024]{1,0:T(8,128)(2,1)} %refs_0_), channel_id=1, source_target_pairs={{0,6},{1,7},{2,0},{3,1},{4,2},{5,3},{6,4},{7,5},{8,14},{9,15},{10,... | collective-permute-start | bytes 3145736 | tf_op jit(solution)/shard_map/ppermute | solution.py:391
  19.3 17.9 %copy-start.14 = (s32[1,16]{1,0:T(1,128)S(1)}, s32[1,16]{1,0:T(1,128)}, u32[]{:S(2)}) copy-start(s32[1,16]{1,0:T(1,128)} %param.29) | copy-start | bytes 196
  19.4 17.9 %copy-start.9 = (s32[1,16]{1,0:T(1,128)S(1)}, s32[1,16]{1,0:T(1,128)}, u32[]{:S(2)}) copy-start(s32[1,16]{1,0:T(1,128)} %param.28) | copy-start | bytes 196
  33.7 20.7 %copy-start.2 = (bf16[4,256,640]{2,1,0:T(8,128)(2,1)S(1)}, bf16[4,256,640]{2,1,0:T(8,128)(2,1)}, u32[]{:S(2)}) copy-start(bf16[4,256,640]{2,1,0:T(8,128)(2,1)} %get-tuple-element.34) | copy-start | bytes 3932164
  36.0 18.4 %copy-start.4 = (bf16[512,1024]{1,0:T(8,128)(2,1)}, bf16[512,1024]{1,0:T(8,128)(2,1)S(1)}, u32[]{:S(2)}) copy-start(bf16[512,1024]{1,0:T(8,128)(2,1)S(1)} %collective-permute-done.refs_1_) | copy-start | bytes 3145732
  37.3 17.1 %collective-permute-start.2 = (bf16[4,256,640]{2,1,0:T(8,128)(2,1)}, bf16[4,256,640]{2,1,0:T(8,128)(2,1)}, u32[]{:S(2)}, u32[]{:S(2)}) collective-permute-start(bf16[4,256,640]{2,1,0:T(8,128)(2,1)} %get-tuple-element.35), channel_id=1, source_target_pairs={{0,1},{1,0},{2,3},{3,2},{4,5},{5,4},{6,7},{7,6},{8,9},{9,8},{10,11... | collective-permute-start | bytes 3932168 | tf_op jit(solution)/shard_map/ppermute | solution.py:394
  37.6 27.5 %collective-permute-start.3 = (bf16[512,1024]{1,0:T(8,128)(2,1)}, bf16[512,1024]{1,0:T(8,128)(2,1)}, u32[]{:S(2)}, u32[]{:S(2)}) collective-permute-start(bf16[512,1024]{1,0:T(8,128)(2,1)} %refs_0_), channel_id=1, source_target_pairs={{0,4},{1,5},{2,6},{3,7},{4,0},{5,1},{6,2},{7,3},{8,12},{9,13},{10,... | collective-permute-start | bytes 3145736 | tf_op jit(solution)/shard_map/ppermute | solution.py:391
  40.6 21.3 %all-to-all-start = ((s32[32,1,8]{2,1,0:T(1,128)}), s32[32,1,8]{2,1,0:T(1,128)S(1)}, u32[]{:S(2)}, u32[]{:S(2)}) async-start(s32[32,1,8]{2,1,0:T(1,128)} %bitcast.10), calls=%async_computation | async-start | bytes 32768 | tf_op jit(solution)/shard_map/all_to_all | solution.py:435
  70.1 7.5 %collective-permute-start.4 = (bf16[2048,1024]{1,0:T(8,128)(2,1)}, bf16[2048,1024]{1,0:T(8,128)(2,1)}, u32[]{:S(2)}, u32[]{:S(2)}) collective-permute-start(bf16[2048,1024]{1,0:T(8,128)(2,1)} %shard_map.213.refs_0_), channel_id=1, source_target_pairs={{0,1},{1,0},{2,3},{3,2},{4,5},{5,4},{6,7},{7,6},{8,9},{9,8},{10,11... | collective-permute-start | bytes 12582920 | tf_op jit(solution)/shard_map/ppermute | solution.py:394
  86.2 5.3 %copy-start.7 = (f32[1280]{0:T(1024)S(1)}, f32[1280]{0:T(1024)}, u32[]{:S(2)}) copy-start(f32[1280]{0:T(1024)} %param.26) | copy-start | bytes 15364
  86.3 5.3 %copy-start.8 = (f32[1280]{0:T(1024)S(1)}, f32[1280]{0:T(1024)}, u32[]{:S(2)}) copy-start(f32[1280]{0:T(1024)} %param.27) | copy-start | bytes 15364
  86.3 5.4 %copy-start.11 = (f32[128]{0:T(128)S(1)}, f32[128]{0:T(128)}, u32[]{:S(2)}) copy-start(f32[128]{0:T(128)} %param.37) | copy-start | bytes 1540
  86.3 5.4 %copy-start.12 = (f32[128]{0:T(128)S(1)}, f32[128]{0:T(128)}, u32[]{:S(2)}) copy-start(f32[128]{0:T(128)} %param.35) | copy-start | bytes 1540
  86.3 19.6 %copy-start.3 = (bf16[256,640]{1,0:T(8,128)(2,1)S(1)}, bf16[256,640]{1,0:T(8,128)(2,1)}, u32[]{:S(2)}) copy-start(bf16[256,640]{1,0:T(8,128)(2,1)} %get-tuple-element.38) | copy-start | bytes 983044
  87.1 10.8 %collective-permute-start.5 = (bf16[256,640]{1,0:T(8,128)(2,1)}, bf16[256,640]{1,0:T(8,128)(2,1)S(1)}, u32[]{:S(2)}, u32[]{:S(2)}) collective-permute-start(bf16[256,640]{1,0:T(8,128)(2,1)} %get-tuple-element.59), channel_id=1, source_target_pairs={{0,2},{1,3},{2,4},{3,5},{4,6},{5,7},{6,0},{7,1},{8,10},{9,11},{10,... | collective-permute-start | bytes 983048 | tf_op jit(solution)/shard_map/ppermute | solution.py:391
  88.2 9.7 %collective-permute-start.6 = (bf16[256,640]{1,0:T(8,128)(2,1)S(1)}, bf16[256,640]{1,0:T(8,128)(2,1)S(1)}, u32[]{:S(2)}, u32[]{:S(2)}) collective-permute-start(bf16[256,640]{1,0:T(8,128)(2,1)S(1)} %get-tuple-element.61), channel_id=1, source_target_pairs={{0,6},{1,7},{2,0},{3,1},{4,2},{5,3},{6,4},{7,5},{8,14},{9,15},{10,... | collective-permute-start | bytes 983048 | tf_op jit(solution)/shard_map/ppermute | solution.py:391
  89.2 16.8 %collective-permute-start.7 = (bf16[256,640]{1,0:T(8,128)(2,1)S(1)}, bf16[256,640]{1,0:T(8,128)(2,1)S(1)}, u32[]{:S(2)}, u32[]{:S(2)}) collective-permute-start(bf16[256,640]{1,0:T(8,128)(2,1)S(1)} %get-tuple-element.60), channel_id=1, source_target_pairs={{0,4},{1,5},{2,6},{3,7},{4,0},{5,1},{6,2},{7,3},{8,12},{9,13},{10,... | collective-permute-start | bytes 983048 | tf_op jit(solution)/shard_map/ppermute | solution.py:391
  106.2 1.2 collective-permute-start.8
  142.6 24.3 %all-to-all-start.2 = ((bf16[8,5,32,256]{3,2,1,0:T(8,128)(2,1)}), bf16[8,5,32,256]{3,2,1,0:T(8,128)(2,1)S(1)}, u32[]{:S(2)}, u32[]{:S(2)}) async-start(bf16[8,5,32,256]{3,2,1,0:T(8,128)(2,1)} %bitcast.58), calls=%async_computation.2 | async-start | bytes 1310720 | tf_op jit(solution)/shard_map/all_to_all | solution.py:484
  166.9 15.7 %copy-start = (bf16[8,5,32,256]{3,2,1,0:T(8,128)(2,1)}, bf16[8,5,32,256]{3,2,1,0:T(8,128)(2,1)S(1)}, u32[]{:S(2)}) copy-start(bf16[8,5,32,256]{3,2,1,0:T(8,128)(2,1)S(1)} %all-to-all-done.2) | copy-start | bytes 1966084
  166.9 24.1 %all-to-all-start.1 = ((bf16[32,16,640]{2,1,0:T(8,128)(2,1)}), bf16[32,16,640]{2,1,0:T(8,128)(2,1)S(1)}, u32[]{:S(2)}, u32[]{:S(2)}) async-start(bf16[32,16,640]{2,1,0:T(8,128)(2,1)} %shard_map.215), calls=%async_computation.1 | async-start | bytes 1310720 | tf_op jit(solution)/shard_map/all_to_all | solution.py:479
  191.0 0.9 copy-start.1
Sparse Core Ops, SparseCore 0:
  10.9 122.6 all-gather.1
